TPU v7x, 1024 devices: a whole 4x4x32 slice. The times are simulated.
1024 devices in a mesh: gx: 8 (over z_hi, core), gy: 16 (over y, x), gz: 8 (over z_lo).
Axes of the slice: x: 4, y: 4, z: 32 (z_hi: 4, z_lo: 8; z = z_hi * 8 + z_lo), core: 2. Of those that a mesh axis runs over, the one named last changes fastest.
Arguments:
- load: float32 [3, 64, 128, 1024], P(None, 'gz', 'gy', 'gx'), may hold values from -30 to 30
- classes: int32 [56, 112, 1016], P('gz', 'gy', 'gx'), may hold values from 0 to 63
- densities: float32 [64], replicated, may hold values from 0.2 to 1
Outputs:
- displacement: float32 [3, 64, 128, 1024], P(None, 'gz', 'gy', 'gx')
- residual: float32 [3, 64, 128, 1024], P(None, 'gz', 'gy', 'gx')
- search_direction: float32 [3, 64, 128, 1024], P(None, 'gz', 'gy', 'gx')
All inputs are finite; a program needn't handle non-finite values.
Results may differ from a plain program's by a relative error of at most 0.0003.
Values sent between devices are 32-bit elements; how exact they have to be, the bound alone decides.
A program may use at most 32 MiB of HBM per device.

v0:
```python
import math

import jax
import jax.numpy as jnp
import numpy as np
from jax import lax
from jax.sharding import PartitionSpec as P

soft_floor = 0.001


def padded(cells, sides, width):
    for axis, dim in sides:
        count = lax.axis_size(axis)
        ends = count - 1
        head = lax.slice_in_dim(cells, 0, width, axis=dim)
        tail = lax.slice_in_dim(cells, cells.shape[dim] - width, cells.shape[dim], axis=dim)
        cells = jnp.concatenate(
            [
                lax.ppermute(tail, axis, [(i, (i + 1) % count) for i in range(ends)]),
                cells,
                lax.ppermute(head, axis, [((i + 1) % count, i) for i in range(ends)]),
            ],
            axis=dim,
        )
    return cells


def element_stiffness():
    poisson = 0.3
    lame_first = poisson / ((1.0 + poisson) * (1.0 - 2.0 * poisson))
    shear = 0.5 / (1.0 + poisson)
    elastic = np.zeros((6, 6))
    elastic[:3, :3] = lame_first
    for axis_index in range(3):
        elastic[axis_index, axis_index] += 2.0 * shear
        elastic[3 + axis_index, 3 + axis_index] = shear
    gauss_points = [0.5 - 0.5 / math.sqrt(3.0), 0.5 + 0.5 / math.sqrt(3.0)]
    matrix = np.zeros((24, 24))
    for point_z in gauss_points:
        for point_y in gauss_points:
            for point_x in gauss_points:
                strain = np.zeros((6, 24))
                for corner in range(8):
                    bit_x = corner % 2
                    bit_y = corner // 2 % 2
                    bit_z = corner // 4
                    shape_x = 1 - bit_x + (2 * bit_x - 1) * point_x
                    shape_y = 1 - bit_y + (2 * bit_y - 1) * point_y
                    shape_z = 1 - bit_z + (2 * bit_z - 1) * point_z
                    grad_x = (2 * bit_x - 1) * shape_y * shape_z
                    grad_y = shape_x * (2 * bit_y - 1) * shape_z
                    grad_z = shape_x * shape_y * (2 * bit_z - 1)
                    column = 3 * corner
                    strain[0, column] = grad_x
                    strain[1, column + 1] = grad_y
                    strain[2, column + 2] = grad_z
                    strain[3, column] = grad_y
                    strain[3, column + 1] = grad_x
                    strain[4, column + 1] = grad_z
                    strain[4, column + 2] = grad_y
                    strain[5, column] = grad_z
                    strain[5, column + 2] = grad_x
                matrix += strain.T @ elastic @ strain / 8.0
    return matrix


def corner_offsets():
    return [(corner // 4, corner // 2 % 2, corner % 2) for corner in range(8)]


def pad_along(values, dim, before, after):
    widths = [(0, 0)] * values.ndim
    widths[dim] = (before, after)
    return jnp.pad(values, widths)


def fold(extended, dim):
    count = extended.shape[dim]
    inner = lax.slice_in_dim(extended, 1, count - 1, axis=dim)
    lowest = lax.slice_in_dim(extended, 0, 1, axis=dim)
    highest = lax.slice_in_dim(extended, count - 1, count, axis=dim)
    return inner + pad_along(lowest, dim, 0, count - 3) + pad_along(highest, dim, count - 3, 0)


def assemble(values):
    extended = padded(values, (("gx", 3), ("gy", 2), ("gz", 1)), 1)
    return fold(fold(fold(extended, 3), 2), 1)


def apply_local(field, stiffness, matrix):
    depth, rows, width = stiffness.shape
    pieces = [
        field[:, bit_z : bit_z + depth, bit_y : bit_y + rows, bit_x : bit_x + width]
        for bit_z, bit_y, bit_x in corner_offsets()
    ]
    gathered = jnp.stack(pieces, 0).reshape(24, depth * rows * width)
    result = jnp.dot(matrix, gathered, precision=lax.Precision.HIGHEST) * stiffness.reshape(
        1, depth * rows * width
    )
    result = result.reshape(8, 3, depth, rows, width)
    total = jnp.zeros(field.shape, jnp.float32)
    for corner, (bit_z, bit_y, bit_x) in enumerate(corner_offsets()):
        total = total + jnp.pad(
            result[corner], ((0, 0), (bit_z, 1 - bit_z), (bit_y, 1 - bit_y), (bit_x, 1 - bit_x))
        )
    return total


def owned(count, axis_name):
    if axis_name == "gx":
        last = lax.axis_index("gx") == lax.axis_size("gx") - 1
    elif axis_name == "gy":
        last = lax.axis_index("gy") == lax.axis_size("gy") - 1
    else:
        last = lax.axis_index("gz") == lax.axis_size("gz") - 1
    return ((jnp.arange(count + 1) < count) | last).astype(jnp.float32)


def on_device(load, classes, densities):
    matrix = jnp.asarray(element_stiffness(), jnp.float32)
    corner_diag = jnp.diagonal(matrix).reshape(8, 3)
    depth, rows, width = classes.shape
    rho = jnp.take(densities, classes)
    stiffness = soft_floor + rho * rho * rho * (1.0 - soft_floor)
    diag_part = jnp.zeros(load.shape, jnp.float32)
    for corner, (bit_z, bit_y, bit_x) in enumerate(corner_offsets()):
        term = corner_diag[corner][:, None, None, None] * stiffness[None]
        diag_part = diag_part + jnp.pad(
            term, ((0, 0), (bit_z, 1 - bit_z), (bit_y, 1 - bit_y), (bit_x, 1 - bit_x))
        )
    summed = assemble(jnp.concatenate([diag_part, load], 0))
    clamped = (jnp.arange(width + 1) == 0) & (lax.axis_index("gx") == 0)
    keep = (1.0 - clamped.astype(jnp.float32))[None, None, None, :]
    diagonal = jnp.where(keep > 0.5, summed[:3], 1.0)
    start = keep * summed[3:]
    preconditioned = start / diagonal
    image = keep * assemble(apply_local(preconditioned, stiffness, matrix))
    weights = (
        owned(depth, "gz")[:, None, None]
        * owned(rows, "gy")[None, :, None]
        * owned(width, "gx")[None, None, :]
    )
    rz_start, curvature = lax.psum(
        (
            jnp.sum(weights[None] * start * preconditioned),
            jnp.sum(weights[None] * preconditioned * image),
        ),
        ("gx", "gy", "gz"),
    )
    alpha = rz_start / curvature
    solution = alpha * preconditioned
    remaining = start - alpha * image
    scaled = remaining / diagonal
    rz_next = lax.psum(jnp.sum(weights[None] * remaining * scaled), ("gx", "gy", "gz"))
    direction = scaled + rz_next / rz_start * preconditioned
    return (solution, remaining, direction)


def solution(mesh):
    in_specs = (P(None, "gz", "gy", "gx"), P("gz", "gy", "gx"), P())
    out_specs = (P(None, "gz", "gy", "gx"), P(None, "gz", "gy", "gx"), P(None, "gz", "gy", "gx"))
    return jax.shard_map(
        on_device, mesh=mesh, in_specs=in_specs, out_specs=out_specs, check_vma=False
    )
```

profile of v0, /device:TPU:1, one launch (start us, length us, event | category | flops | bytes accessed | tf_op | source)
XLA Modules:
  0.0 463.2 jit_solution(8951357611959574583)
XLA Ops:
  1.4 0.8 gather_fusion
  2.4 35.3 %gather_fusion.1 = f32[6223]{0:T(1024)S(1)} fusion(f32[64]{0:T(128)S(1)} %copy-done, s32[7168]{0:T(1024)S(1)} %pad_clamp_fusion), kind=kCustom, calls=%fused_computation.1 | custom fusion | bytes 74676 | tf_op jit(solution)/shard_map/jit(_take)/gather | solution.py:124
  38.1 0.7 copy-done.2
  39.0 16.8 %collective-permute-start = (f32[6,8,8,1]{3,2,1,0:T(8,128)S(1)}, f32[6,8,8,1]{3,2,1,0:T(8,128)S(1)}, u32[]{:S(2)}, u32[]{:S(2)}) collective-permute-start(f32[6,8,8,1]{3,2,1,0:T(8,128)S(1)} %get-tuple-element.27), channel_id=1, source_target_pairs={{0,128},{128,256},{256,384},{384,512},{512,640},{640,768},{768,896... | collective-permute-start | bytes 4616 | tf_op jit(solution)/shard_map/ppermute | solution.py:20
  55.8 1.9 collective-permute-start.1
  58.4 26.2 %collective-permute-done.1 = f32[6,8,8,1]{3,2,1,0:T(8,128)S(1)} collective-permute-done((f32[6,8,8,1]{3,2,1,0:T(8,128)S(1)}, f32[6,8,8,1]{3,2,1,0:T(8,128)S(1)}, u32[]{:S(2)}, u32[]{:S(2)}) %collective-permute-start.1) | collective-permute-done | bytes 1568 | tf_op jit(solution)/shard_map/ppermute | solution.py:22
  85.0 3.1 collective-permute-start.2
  88.1 1.3 collective-permute-start.3
  89.4 3.5 collective-permute-done.3
  93.1 2.0 collective-permute-start.4
  95.1 1.3 collective-permute-start.5
  96.7 3.7 collective-permute-done.5
  105.5 4.6 collective-permute-start.6
  110.2 1.9 collective-permute-start.7
  112.2 17.5 %collective-permute-done.7 = f32[3,8,8,1]{3,2,1,0:T(8,128)S(1)} collective-permute-done((f32[3,8,8,1]{3,2,1,0:T(8,128)S(1)}, f32[3,8,8,1]{3,2,1,0:T(8,128)S(1)}, u32[]{:S(2)}, u32[]{:S(2)}) %collective-permute-start.7) | collective-permute-done | bytes 800 | tf_op jit(solution)/shard_map/ppermute | solution.py:22
  129.9 3.1 collective-permute-start.8
  133.0 1.3 collective-permute-start.9
  134.3 3.2 collective-permute-done.9
  137.7 1.3 collective-permute-start.10
  139.0 1.3 collective-permute-start.11
  140.4 3.5 collective-permute-done.11
  145.2 161.8 %all-reduce.22 = (f32[]{:T(128)}, f32[]{:T(128)}) all-reduce(f32[]{:T(128)} %get-tuple-element.4, f32[]{:T(128)} %get-tuple-element.3), channel_id=1, replica_groups=mesh['gx'=8,'gy'=16,'gz'=8] {'gx','gy','gz'}, use_global_device_ids=true, to_apply=%region_1.2 | all-reduce | flops 2 | bytes 16 | tf_op jit(solution)/shard_map/psum | solution.py:144
  309.1 152.0 %psum.23 = f32[]{:T(128)} all-reduce(f32[]{:T(128)} %get-tuple-element.7), channel_id=1, replica_groups=mesh['gx'=8,'gy'=16,'gz'=8] {'gx','gy','gz'}, use_global_device_ids=true, to_apply=%region_5.6 | all-reduce | flops 1 | bytes 8 | tf_op jit(solution)/shard_map/psum | solution.py:155
  462.5 0.7 multiply_add_fusion
  (78 shorter events, 10.3 us)
Async XLA Ops:
  0.6 1.8 copy-start
  0.6 0.7 copy-start.1
  1.4 0.9 copy-start.4
  37.9 0.9 copy-start.2
  39.0 19.4 %collective-permute-start = (f32[6,8,8,1]{3,2,1,0:T(8,128)S(1)}, f32[6,8,8,1]{3,2,1,0:T(8,128)S(1)}, u32[]{:S(2)}, u32[]{:S(2)}) collective-permute-start(f32[6,8,8,1]{3,2,1,0:T(8,128)S(1)} %get-tuple-element.27), channel_id=1, source_target_pairs={{0,128},{128,256},{256,384},{384,512},{512,640},{640,768},{768,896... | collective-permute-start | bytes 4616 | tf_op jit(solution)/shard_map/ppermute | solution.py:20
  55.8 28.8 %collective-permute-start.1 = (f32[6,8,8,1]{3,2,1,0:T(8,128)S(1)}, f32[6,8,8,1]{3,2,1,0:T(8,128)S(1)}, u32[]{:S(2)}, u32[]{:S(2)}) collective-permute-start(f32[6,8,8,1]{3,2,1,0:T(8,128)S(1)} %get-tuple-element.28), channel_id=1, source_target_pairs={{128,0},{256,128},{384,256},{512,384},{640,512},{768,640},{896,768... | collective-permute-start | bytes 4616 | tf_op jit(solution)/shard_map/ppermute | solution.py:22
  85.0 4.4 collective-permute-start.2
  88.1 4.8 %collective-permute-start.3 = (f32[6,8,1,130]{3,2,1,0:T(1,128)S(1)}, f32[6,8,1,130]{3,2,1,0:T(1,128)S(1)}, u32[]{:S(2)}, u32[]{:S(2)}) collective-permute-start(f32[6,8,1,130]{3,2,1,0:T(1,128)S(1)} %get-tuple-element.22), channel_id=1, source_target_pairs={{8,0},{16,8},{24,16},{32,24},{40,32},{48,40},{56,48},{64,56},{72,6... | collective-permute-start | bytes 74888 | tf_op jit(solution)/shard_map/ppermute | solution.py:22
  93.1 3.6 collective-permute-start.4
  95.1 5.4 %collective-permute-start.5 = (f32[6,1,10,130]{3,2,1,0:T(8,128)S(1)}, f32[6,1,10,130]{3,2,1,0:T(8,128)S(1)}, u32[]{:S(2)}, u32[]{:S(2)}) collective-permute-start(f32[6,1,10,130]{3,2,1,0:T(8,128)S(1)} %get-tuple-element.12), channel_id=1, source_target_pairs={{1,0},{2,1},{3,2},{4,3},{5,4},{6,5},{7,6},{9,8},{10,9},{11,10},{12... | collective-permute-start | bytes 93608 | tf_op jit(solution)/shard_map/ppermute | solution.py:22
  100.9 0.7 copy-start.6
  101.8 0.7 copy-start.5
  105.5 6.6 %collective-permute-start.6 = (f32[3,8,8,1]{3,2,1,0:T(8,128)S(1)}, f32[3,8,8,1]{3,2,1,0:T(8,128)S(1)}, u32[]{:S(2)}, u32[]{:S(2)}) collective-permute-start(f32[3,8,8,1]{3,2,1,0:T(8,128)S(1)} %get-tuple-element.31), channel_id=1, source_target_pairs={{0,128},{128,256},{256,384},{384,512},{512,640},{640,768},{768,896... | collective-permute-start | bytes 2312 | tf_op jit(solution)/shard_map/ppermute | solution.py:20
  110.2 19.5 %collective-permute-start.7 = (f32[3,8,8,1]{3,2,1,0:T(8,128)S(1)}, f32[3,8,8,1]{3,2,1,0:T(8,128)S(1)}, u32[]{:S(2)}, u32[]{:S(2)}) collective-permute-start(f32[3,8,8,1]{3,2,1,0:T(8,128)S(1)} %get-tuple-element.32), channel_id=1, source_target_pairs={{128,0},{256,128},{384,256},{512,384},{640,512},{768,640},{896,768... | collective-permute-start | bytes 2312 | tf_op jit(solution)/shard_map/ppermute | solution.py:22
  129.9 4.4 collective-permute-start.8
  133.0 4.6 collective-permute-start.9
  137.7 2.7 collective-permute-start.10
  139.0 4.8 %collective-permute-start.11 = (f32[3,1,10,130]{3,2,1,0:T(8,128)S(1)}, f32[3,1,10,130]{3,2,1,0:T(8,128)S(1)}, u32[]{:S(2)}, u32[]{:S(2)}) collective-permute-start(f32[3,1,10,130]{3,2,1,0:T(8,128)S(1)} %get-tuple-element.24), channel_id=1, source_target_pairs={{1,0},{2,1},{3,2},{4,3},{5,4},{6,5},{7,6},{9,8},{10,9},{11,10},{12... | collective-permute-start | bytes 46808 | tf_op jit(solution)/shard_map/ppermute | solution.py:22
  309.1 154.1 %copy-start.3 = (f32[3,8,8,128]{3,2,1,0:T(8,128)}, f32[3,8,8,128]{3,2,1,0:T(8,128)S(1)}, u32[]{:S(2)}) copy-start(f32[3,8,8,128]{3,2,1,0:T(8,128)S(1)} %get-tuple-element.8) | copy-start | bytes 294916
where the time goes:
time: 464 us; the launch traced here: 463 us
  blocking collectives  314 us (68%)
  waiting for transfers between devices  58.4 us (13%)
  local copies, waits for them, and re-layouts  41.2 us (9%)
  starting transfers between devices  40 us (9%)
  other arithmetic  5.16 us (1%)
    psum x1, blocking collectives, on_device(): lax.psum((jnp.sum(weights[None] * start * preconditioned), jnp.sum(weight...  162 us
    psum x1, blocking collectives, on_device(): lax.psum(jnp.sum(weights[None] * remaining * scaled), ('gx', 'gy', 'gz'))  152 us
    ppermute x6, waiting for transfers between devices, padded(): lax.ppermute(head, axis, [((i + 1) % count, i) for i in range(ends)])  57.6 us
    gather x2, local copies, waits for them, and re-layouts, on_device(): rho = jnp.take(densities, classes)  35.4 us
    ppermute x6, starting transfers between devices, padded(): lax.ppermute(tail, axis, [(i, (i + 1) % count) for i in range(ends)])  31 us
  transfers between devices with their start and end apart: 12, of which 8 were waited for; matrix products, arithmetic and copies ran while one was open for 0% of the time, Pallas kernels for 0%

commit v1 on v0

v1 whole, which is shorter than its diff:
```python
import functools
import math

import jax
import jax.numpy as jnp
import numpy as np
from jax import lax
from jax.experimental import pallas as pl
from jax.experimental.pallas import tpu as pltpu
from jax.sharding import PartitionSpec as P

MESH = pl.DeviceIdType.MESH
soft_floor = 0.001
poisson = 0.3
lame = poisson / ((1.0 + poisson) * (1.0 - 2.0 * poisson))
shear = 0.5 / (1.0 + poisson)

MASS = (0.25, 1.0 / 12.0)
MODES = [(mx, my, mz) for mx in (0, 1) for my in (0, 1) for mz in (0, 1)]


def mode_couplings():
    rows = {(c, m): [] for c in range(3) for m in MODES}
    for c in range(3):
        for m in MODES:
            own = 0.0
            for axis in range(3):
                if m[axis] == 1:
                    factor = lame + 2.0 * shear if axis == c else shear
                    others = [MASS[m[o]] for o in range(3) if o != axis]
                    own += factor * others[0] * others[1]
            if own:
                rows[c, m].append((own, c, m))
            for k in range(3):
                if k == c:
                    continue
                rest = 3 - c - k
                if m[c] == 1 and m[k] == 0:
                    factor = lame
                elif m[c] == 0 and m[k] == 1:
                    factor = shear
                else:
                    continue
                partner = list(m)
                partner[c], partner[k] = m[k], m[c]
                rows[c, m].append((factor * 0.25 * MASS[m[rest]], k, tuple(partner)))
    return rows


COUPLINGS = mode_couplings()
CORNER_DIAGONAL = sum(w for m in MODES for w, c, _ in COUPLINGS[0, m] if c == 0)


def kernel(
    shape,
    load_hbm, classes_hbm, densities_hbm,
    displacement_ref, residual_ref, direction_ref,
    load_v, classes_v, table_v, cells_v,
    S, ZL, ZU, YH, YLO, YL, YU, CLL, CLU, CUL, CUU,
    A, G, XT, TL, TR, XM, IM, INV, FZ, FYS, FY, FYZ, FXS, FX,
    RA, RB, RC, rows_v,
    in_sem, y_send, y_recv, x_send, x_recv, f_send, f_recv, a_send, a_recv,
):
    NGX, NGY, NGZ = shape
    ring = NGX // 2 * NGZ
    reach = ring // 4
    gx, gy, gz = (lax.axis_index(a) for a in ("gx", "gy", "gz"))
    core = lax.rem(gx, 2)
    along = lax.div(gx, 2) * NGZ + gz
    has = {
        ("z", -1): gz > 0, ("z", 1): gz < NGZ - 1,
        ("y", -1): gy > 0, ("y", 1): gy < NGY - 1,
        ("x", -1): gx > 0, ("x", 1): gx < NGX - 1,
    }

    def both(dy, dz):
        terms = []
        if dy:
            terms.append(has["y", dy])
        if dz:
            terms.append(has["z", dz])
        return terms[0] if len(terms) == 1 else jnp.logical_and(terms[0], terms[1])

    def ring_device(offset, flip):
        q = lax.rem(along + offset + ring, ring)
        c = 1 - core if flip else core
        return {"gx": lax.div(q, NGZ) * 2 + c, "gy": gy, "gz": lax.rem(q, NGZ)}

    def row_device(offset):
        return {"gx": gx, "gy": lax.rem(gy + offset, NGY), "gz": gz}

    def block_device(dx, dy, dz):
        return {"gx": gx + dx, "gy": gy + dy, "gz": gz + dz}

    window = [o for o in range(-(reach - 1), reach + 1) if o != 0]
    sides = [(dy, dz) for dy in (-1, 0, 1) for dz in (-1, 0, 1) if (dy, dz) != (0, 0)]
    side_buffer = {
        (0, -1): ZL, (0, 1): ZU, (-1, 0): YL, (1, 0): YU,
        (-1, -1): CLL, (-1, 1): CLU, (1, -1): CUL, (1, 1): CUU,
    }

    for (dy, dz), buffer in side_buffer.items():
        @pl.when(jnp.logical_not(both(dy, dz)))
        def _(buffer=buffer):
            buffer[...] = jnp.zeros_like(buffer)
    for dx, buffer in ((-1, TL), (1, TR)):
        @pl.when(jnp.logical_not(has["x", dx]))
        def _(buffer=buffer):
            buffer[...] = jnp.zeros_like(buffer)

    barrier = pltpu.get_barrier_semaphore()

    def tell(device):
        pl.semaphore_signal(barrier, inc=1, device_id=device, device_id_type=MESH)

    awaited = jnp.int32(0)
    for offset in (-reach, reach):
        for flip in (False, True):
            tell(ring_device(offset, flip))
            awaited = awaited + 1
    for dx in (-1, 1):
        @pl.when(has["x", dx])
        def _(dx=dx):
            tell(block_device(dx, 0, 0))
        awaited = awaited + has["x", dx].astype(jnp.int32)
    for offset in sorted(window, key=lambda o: -abs(o)):
        if abs(offset) != reach:
            tell(ring_device(-offset, False))
            awaited = awaited + 1
    for offset in range(1, NGY):
        tell(row_device(offset))
        awaited = awaited + 1
    for dy, dz in sides:
        if True:
            @pl.when(both(dy, dz))
            def _(dy=dy, dz=dz):
                tell(block_device(0, dy, dz))
            awaited = awaited + both(dy, dz).astype(jnp.int32)

    loads = [
        pltpu.make_async_copy(classes_hbm, classes_v, in_sem.at[0]),
        pltpu.make_async_copy(densities_hbm, table_v.at[:, pl.ds(0, 128)], in_sem.at[1]),
        pltpu.make_async_copy(load_hbm, load_v, in_sem.at[2]),
    ]
    for copy in loads:
        copy.start()

    lane = lax.broadcasted_iota(jnp.int32, (8, 128), 1)
    sub = lax.broadcasted_iota(jnp.int32, (8, 128), 0)
    lane1 = lax.broadcasted_iota(jnp.int32, (1, 128), 1)
    third, third1 = lax.div(lane, 3), lax.div(lane1, 3)

    def roll(v, shift, axis):
        return pltpu.roll(v, shift % v.shape[axis], axis)

    cells_v[...] = jnp.zeros_like(cells_v)
    loads[0].wait()
    cells_v[:, 0:7, 0:127] = classes_v[...]
    loads[1].wait()
    rho = table_v[...]
    table = jnp.broadcast_to(soft_floor + rho * rho * rho * (1.0 - soft_floor), (8, 128))
    inside = jnp.logical_and(sub < 7, lane < 127)
    previous = jnp.zeros((8, 128), jnp.float32)
    for z in range(8):
        if z < 7:
            picked = jnp.take_along_axis(table, cells_v[z], axis=1, mode="promise_in_bounds")
            s = jnp.where(inside, picked, 0.0)
        else:
            s = jnp.zeros((8, 128), jnp.float32)
        S[z, 4] = s
        s = s + roll(s, 1, 1)
        s = s + roll(s, 1, 0)
        S[z, 3] = s + previous
        previous = s
    loads[2].wait()
    for z in range(8):
        for c in range(3):
            S[z, c] = load_v[c, z]
    for f in range(4):
        YH[f] = jnp.concatenate([S[z, f, 7:8, :] for z in range(8)], axis=0)
        YLO[f] = jnp.concatenate([S[z, f, 0:1, :] for z in range(8)], axis=0)
        YLO[4 + f] = jnp.concatenate([S[z, f, 1:2, :] for z in range(8)], axis=0)
    YLO[8] = jnp.concatenate([S[z, 4, 0:1, :] for z in range(8)], axis=0)

    pl.semaphore_wait(barrier, awaited)

    def remote(source, target, sends, recvs, index, device):
        return pltpu.make_async_remote_copy(
            src_ref=source, dst_ref=target, send_sem=sends.at[index], recv_sem=recvs.at[index],
            device_id=device, device_id_type=MESH,
        )

    source_of = {
        (0, -1): S.at[pl.ds(0, 2)],
        (0, 1): S.at[7, pl.ds(0, 4)],
        (-1, 0): YLO,
        (1, 0): YH,
        (-1, -1): YLO.at[:, pl.ds(0, 2)],
        (-1, 1): YLO.at[pl.ds(0, 8), pl.ds(7, 1)],
        (1, -1): YH.at[:, pl.ds(0, 2)],
        (1, 1): YH.at[:, pl.ds(7, 1)],
    }
    y_copies = {
        (dy, dz): remote(source_of[dy, dz], side_buffer[-dy, -dz], y_send, y_recv, sides.index((dy, dz)), block_device(0, dy, dz))
        for dy, dz in sides
    }
    for dy, dz in sorted(sides, key=lambda side: -abs(side[0]) - abs(side[1])):
        @pl.when(both(dy, dz))
        def _(copy=y_copies[dy, dz]):
            copy.start()
    for dy, dz in sides:
        @pl.when(both(dy, dz))
        def _(copy=y_copies[-dy, -dz]):
            copy.wait_recv()

    def wide(tile):
        return jnp.broadcast_to(tile, (8, 128))

    top, bottom = sub == 0, sub == 7
    for f in range(4):
        low = YL[f] + jnp.where(top, wide(CLL[f]), 0.0) + jnp.where(bottom, wide(CLU[f, 0:1]), 0.0)
        low8 = CLU[f, 1:2]
        high = YU[f] + jnp.where(top, wide(CUL[f]), 0.0) + jnp.where(bottom, wide(CUU[f, 0:1]), 0.0)
        high8 = CUU[f, 1:2]
        G[f, 0:8] = YU[4 + f] + jnp.where(top, wide(CUL[4 + f]), 0.0) + jnp.where(bottom, wide(CUU[4 + f, 0:1]), 0.0)
        G[f, 8:9] = CUU[4 + f, 1:2]
        for z in range(9):
            tile = S[z, f] if z < 8 else ZU[1, f]
            if z == 0:
                tile = tile + ZL[f]
            if z == 7:
                tile = tile + ZU[0, f]
            lower = low[z : z + 1] if z < 8 else low8
            upper = high[z : z + 1] if z < 8 else high8
            A[z, f] = tile + jnp.where(top, wide(lower), 0.0) + jnp.where(bottom, wide(upper), 0.0)
    edge = YU[8]
    for z in range(8):
        tile = S[z, 4] if z < 7 else ZU[0, 4]
        row = edge[z : z + 1] if z < 7 else CUU[8, 0:1]
        A[z, 4] = jnp.where(bottom, wide(row), tile)

    packed = jnp.zeros((8, 128), jnp.float32)
    for f in range(4):
        for z in range(9):
            k = 9 * f + z
            packed = jnp.where(third == k, roll(A[z, f], 3 * k - 127, 1), packed)
        packed = jnp.where(third == 36 + f, roll(G[f, 0:8], 3 * (36 + f) - 127, 1), packed)
    for z in range(8):
        packed = jnp.where(lane == 120 + z, roll(A[z, 4], 120 + z, 1), packed)
    XT[0:8] = packed
    packed8 = jnp.zeros((1, 128), jnp.float32)
    for f in range(4):
        packed8 = jnp.where(third1 == f, roll(G[f, 8:9], 3 * f - 127, 1), packed8)
    XT[8:9] = packed8
    XT[9:16] = jnp.zeros((7, 128), jnp.float32)

    to_right = remote(XT, TL, x_send, x_recv, 0, block_device(1, 0, 0))
    to_left = remote(XT, TR, x_send, x_recv, 1, block_device(-1, 0, 0))

    @pl.when(has["x", 1])
    def _():
        to_right.start()

    @pl.when(has["x", -1])
    def _():
        to_left.start()

    @pl.when(has["x", -1])
    def _():
        to_right.wait_recv()

    @pl.when(has["x", 1])
    def _():
        to_left.wait_recv()

    def merged(left, right, lanes):
        return jnp.where(lax.rem(lanes, 3) == 2, roll(left, 2, 1), right)

    left_tile, right_tile = TL[0:8], TR[0:8]
    left_row, right_row = TL[8:9], TR[8:9]
    tile_in = merged(left_tile, right_tile, lane)
    row_in = merged(left_row, right_row, lane1)
    ends = jnp.logical_or(lane == 0, lane == 127)
    ends1 = jnp.logical_or(lane1 == 0, lane1 == 127)
    keep = jnp.logical_or(lane > 0, gx > 0)
    keep1 = jnp.logical_or(lane1 > 0, gx > 0)

    def inverse(d):
        return 1.0 / jnp.where(d > 0.0, d * CORNER_DIAGONAL, 1.0)

    d_tile = jnp.where(lane < 27, roll(right_tile, -81, 1), jnp.where(lane < 54, roll(right_tile, -54, 1), roll(right_tile, -27, 1)))
    d_side = jnp.where(third == 36, roll(right_tile, -9, 1), jnp.where(third == 37, roll(right_tile, -6, 1), roll(right_tile, -3, 1)))
    past = right_tile * inverse(jnp.where(lane >= 108, d_side, d_tile))
    d_row = jnp.where(third1 == 0, roll(right_row, -9, 1), jnp.where(third1 == 1, roll(right_row, -6, 1), roll(right_row, -3, 1)))
    past_row = right_row * inverse(d_row)

    def start_tile(value, incoming, k, ends_, keep_):
        value = value + jnp.where(ends_, roll(incoming, 126 - 3 * k, 1), 0.0)
        return jnp.where(keep_, value, 0.0)

    def shifted(p, incoming, k):
        lanes = lax.broadcasted_iota(jnp.int32, p.shape, 1)
        return jnp.where(lanes == 127, roll(incoming, 125 - 3 * k, 1), roll(p, -1, 1))

    inv_side = inverse(start_tile(G[3, 0:8], tile_in, 39, ends, keep))
    inv_corner = inverse(start_tile(G[3, 8:9], row_in, 3, ends1, keep1))
    side, corner = [], []
    for c in range(3):
        p = start_tile(G[c, 0:8], tile_in, 36 + c, ends, keep) * inv_side
        q = shifted(p, past, 36 + c)
        side.append((p + q, q - p))
        p = start_tile(G[c, 8:9], row_in, c, ends1, keep1) * inv_corner
        q = shifted(p, past_row, c)
        corner.append((p + q, q - p))
    owned = jnp.logical_and(jnp.logical_or(lane > 0, gx == 0), jnp.logical_or(sub > 0, gy == 0))
    rz = jnp.zeros((8, 128), jnp.float32)
    for z in range(9):
        inv = inverse(start_tile(A[z, 3], tile_in, 27 + z, ends, keep))
        INV[z] = inv
        for c in range(3):
            start = start_tile(A[z, c], tile_in, 9 * c + z, ends, keep)
            p = start * inv
            if z < 8:
                A[z, c] = start
                rz_mask = jnp.logical_and(owned, gz == 0) if z == 0 else owned
                rz = rz + jnp.where(rz_mask, start * p, 0.0)
            q = shifted(p, past, 9 * c + z)
            sums = (p + q, q - p)
            for m in range(2):
                XM[z, c, m, 0:8] = sums[m]
                XM[z, c, m, 8:9] = side[c][m][z : z + 1] if z < 8 else corner[c][m]

    def plane_modes(z):
        modes = {}
        for c in range(3):
            for mx in range(2):
                here, above = XM[z, c, mx, 0:8], XM[z, c, mx, 1:9]
                modes[c, mx, 0] = here + above
                modes[c, mx, 1] = above - here
        return modes

    def spread(first, second, axis, mask):
        return first - second + jnp.where(mask, roll(first + second, 1, axis), 0.0)

    def to_nodes(plane):
        tiles = []
        for c in range(3):
            rows = [spread(plane[c, mx, 0], plane[c, mx, 1], 0, sub > 0) for mx in range(2)]
            tiles.append(spread(rows[0], rows[1], 1, lane > 0))
        return tiles

    curvature = jnp.zeros((8, 128), jnp.float32)
    square = jnp.zeros((8, 128), jnp.float32)
    lower = plane_modes(0)
    carried = None
    for z in range(8):
        upper = plane_modes(z + 1)
        u = {}
        for key in lower:
            u[key + (0,)] = lower[key] + upper[key]
            u[key + (1,)] = upper[key] - lower[key]
        s = A[z, 4]
        if z < 7 or True:
            s = jnp.where(lane == 127, roll(right_tile, 7 - z, 1), s)
        f = {}
        for c in range(3):
            for m in MODES:
                total = None
                for weight, k, partner in COUPLINGS[c, m]:
                    term = u[(k,) + partner] * weight
                    total = term if total is None else total + term
                f[(c,) + m] = None if total is None else total * s
        plane, carry = {}, {}
        for c in range(3):
            for mx in range(2):
                for my in range(2):
                    first, second = f[c, mx, my, 0], f[c, mx, my, 1]
                    if first is None:
                        plane[c, mx, my], carry[c, mx, my] = -second, second
                    else:
                        plane[c, mx, my], carry[c, mx, my] = first - second, first + second
        if carried is not None:
            plane = {key: plane[key] + carried[key] for key in plane}
        carried = carry
        lower = upper
        inv = INV[z]
        mask = jnp.logical_and(owned, gz == 0) if z == 0 else owned
        for c, image in enumerate(to_nodes(plane)):
            image = jnp.where(keep, image, 0.0)
            IM[z, c] = image
            scaled = image * inv
            curvature = curvature + jnp.where(mask, A[z, c] * scaled, 0.0)
            square = square + jnp.where(mask, image * scaled, 0.0)

    def total_of(tile):
        return jnp.sum(jnp.sum(tile, axis=0, keepdims=True), axis=1, keepdims=True)

    row = jnp.where(lane1 == 0, total_of(rz), jnp.where(lane1 == 1, total_of(curvature), total_of(square)))

    rows_v[0:1] = row
    RA[0:1] = row
    for k in range(1, NGY):
        remote(rows_v.at[pl.ds(0, 1)], RA.at[pl.ds(k, 1)], a_send, a_recv, 0, row_device(k)).start()

    for c in range(3):
        FYS[c] = jnp.concatenate([IM[z, c, 7:8, :] for z in range(8)], axis=0)
    z_fix = remote(IM.at[7], FZ, f_send, f_recv, 0, block_device(0, 0, 1))
    y_fix = remote(FYS, FY, f_send, f_recv, 1, block_device(0, 1, 0))
    yz_fix = remote(FYS.at[:, pl.ds(7, 1)], FYZ, f_send, f_recv, 2, block_device(0, 1, 1))
    for copy, dy, dz in ((yz_fix, 1, 1), (y_fix, 1, 0), (z_fix, 0, 1)):
        @pl.when(both(dy, dz))
        def _(copy=copy):
            copy.start()

    def drain(ref, count, semaphore):
        block = ref.at[pl.ds(0, count)]
        pltpu.make_async_copy(block, block, semaphore).wait()

    drain(RA, NGY - 1, a_recv.at[0])
    row = jnp.sum(RA[...], axis=0, keepdims=True)
    rows_v[1:2] = row
    RB[0:1] = row
    for k, offset in enumerate(window):
        remote(rows_v.at[pl.ds(1, 1)], RB.at[pl.ds(k + 1, 1)], a_send, a_recv, 1, ring_device(offset, False)).start()

    for copy, dy, dz in ((z_fix, 0, -1), (y_fix, -1, 0), (yz_fix, -1, -1)):
        @pl.when(both(dy, dz))
        def _(copy=copy):
            copy.wait_recv()

    @pl.when(both(1, 0))
    def _():
        y_fix.wait_send()

    @pl.when(both(0, 1))
    def _():
        z_fix.wait_send()

    @pl.when(both(1, 1))
    def _():
        yz_fix.wait_send()

    @pl.when(has["z", -1])
    def _():
        IM[0] = FZ[...]

    @pl.when(has["y", -1])
    def _():
        for c in range(3):
            for z in range(8):
                IM[z, c, 0:1, :] = FY[c, z : z + 1, :]

    @pl.when(both(-1, -1))
    def _():
        for c in range(3):
            IM[0, c, 0:1, :] = FYZ[c]

    packed = jnp.zeros((8, 128), jnp.float32)
    for c in range(3):
        for z in range(8):
            k = 8 * c + z
            packed = jnp.where(lane == k, roll(IM[z, c], k - 127, 1), packed)
    FXS[...] = packed
    x_fix = remote(FXS, FX, f_send, f_recv, 3, block_device(1, 0, 0))

    @pl.when(has["x", 1])
    def _():
        x_fix.start()

    drain(RB, len(window), a_recv.at[1])
    row = jnp.sum(RB[...], axis=0, keepdims=True)
    rows_v[2:3] = row
    for k, (offset, flip) in enumerate(((-reach, False), (-reach, True), (reach, False), (reach, True))):
        remote(rows_v.at[pl.ds(2, 1)], RC.at[pl.ds(k, 1)], a_send, a_recv, 2, ring_device(offset, flip)).start()

    for dy, dz in sides:
        @pl.when(both(dy, dz))
        def _(copy=y_copies[dy, dz]):
            copy.wait_send()

    @pl.when(has["x", 1])
    def _():
        to_right.wait_send()
        x_fix.wait_send()

    @pl.when(has["x", -1])
    def _():
        to_left.wait_send()
        x_fix.wait_recv()
        fixed = FX[...]
        for c in range(3):
            for z in range(8):
                IM[z, c] = jnp.where(lane == 0, roll(fixed, -(8 * c + z), 1), IM[z, c])

    drain(RA, NGY - 1, a_send.at[0])
    drain(RB, len(window), a_send.at[1])
    drain(RC, 4, a_recv.at[2])
    row = jnp.sum(RC[0:4], axis=0, keepdims=True)
    rz, curvature, square = (row[:, i : i + 1] for i in range(3))
    alpha = rz / curvature
    beta = alpha * alpha * square / rz - 1.0
    alpha, beta = wide(alpha), wide(beta)
    for z in range(8):
        inv = INV[z]
        for c in range(3):
            start = A[z, c]
            p = start * inv
            residual = start - alpha * IM[z, c]
            displacement_ref[c, z] = alpha * p
            residual_ref[c, z] = residual
            direction_ref[c, z] = residual * inv + beta * p
    drain(RC, 4, a_send.at[2])


def on_device(shape, load, classes, densities):
    f32, i32 = jnp.float32, jnp.int32
    ring = shape[0] // 2 * shape[2]
    count_b = 2 * (ring // 4)
    dma = pltpu.SemaphoreType.DMA

    def rows(n):
        return pltpu.VMEM((-(-n // 8) * 8, 128), f32)

    table = jnp.pad(densities, (0, 64)).reshape(1, 128)
    out = jax.ShapeDtypeStruct(load.shape, f32)
    return pl.pallas_call(
        functools.partial(kernel, shape),
        out_shape=(out, out, out),
        in_specs=[pl.BlockSpec(memory_space=pl.ANY)] * 3,
        out_specs=(pl.BlockSpec(memory_space=pltpu.VMEM),) * 3,
        scratch_shapes=[
            pltpu.VMEM(load.shape, f32), pltpu.VMEM(classes.shape, i32), pltpu.VMEM((1, 128), f32), pltpu.VMEM((7, 8, 128), i32),
            pltpu.VMEM((8, 5, 8, 128), f32), pltpu.VMEM((4, 8, 128), f32), pltpu.VMEM((2, 5, 8, 128), f32),
            pltpu.VMEM((4, 8, 128), f32), pltpu.VMEM((9, 8, 128), f32), pltpu.VMEM((4, 8, 128), f32), pltpu.VMEM((9, 8, 128), f32),
            pltpu.VMEM((4, 1, 128), f32), pltpu.VMEM((4, 2, 128), f32), pltpu.VMEM((8, 1, 128), f32), pltpu.VMEM((9, 2, 128), f32),
            pltpu.VMEM((9, 5, 8, 128), f32), pltpu.VMEM((4, 16, 128), f32),
            pltpu.VMEM((16, 128), f32), pltpu.VMEM((16, 128), f32), pltpu.VMEM((16, 128), f32),
            pltpu.VMEM((9, 3, 2, 16, 128), f32), pltpu.VMEM((8, 3, 8, 128), f32), pltpu.VMEM((9, 8, 128), f32),
            pltpu.VMEM((3, 8, 128), f32), pltpu.VMEM((3, 8, 128), f32), pltpu.VMEM((3, 8, 128), f32), pltpu.VMEM((3, 1, 128), f32),
            pltpu.VMEM((8, 128), f32), pltpu.VMEM((8, 128), f32),
            pltpu.VMEM((shape[1], 128), f32), pltpu.VMEM((count_b, 128), f32), rows(4), rows(3),
            dma((3,)), dma((8,)), dma((8,)), dma((2,)), dma((2,)), dma((4,)), dma((4,)), dma((3,)), dma((3,)),
        ],
        compiler_params=pltpu.CompilerParams(collective_id=0, has_side_effects=True),
        name="step",
    )(load, classes, table)


def solution(mesh):
    shape = tuple(mesh.shape[a] for a in ("gx", "gy", "gz"))
    spec = P(None, "gz", "gy", "gx")
    return jax.shard_map(
        functools.partial(on_device, shape), mesh=mesh,
        in_specs=(spec, P("gz", "gy", "gx"), P()), out_specs=(spec, spec, spec), check_vma=False,
    )
```

time: 464 us -> 61.2 us (0.13)
  blocking collectives: 314 us -> 0 us
  waiting for transfers between devices: 58.4 us -> 0 us
  Pallas kernels: 0 us -> 56 us
  starting transfers between devices: 40 us -> 0 us
  local copies, waits for them, and re-layouts: 41.2 us -> 4.31 us
  other arithmetic: 5.16 us -> 0 us
    psum x2 -> x0, blocking collectives: 314 us -> none  [the longest x1 162 us: on_device(): lax.psum((jnp.sum(weights[None] * start * preconditioned), jnp.sum(weight...]
    ppermute x12 -> x0, waiting for transfers between devices: 58.4 us -> none  [the longest x6 57.6 us: padded(): lax.ppermute(head, axis, [((i + 1) % count, i) for i in range(ends)])]
    pallas_call x0 -> x1, Pallas kernels: none -> 56 us  [on_device(): pl.pallas_call(functools.partial(kernel, shape), out_shape=(out, out, out...]
    ppermute x12 -> x0, starting transfers between devices: 40 us -> none  [the longest x6 31 us: padded(): lax.ppermute(tail, axis, [(i, (i + 1) % count) for i in range(ends)])]
    gather x3 -> x0, local copies, waits for them, and re-layouts: 36.2 us -> none  [the longest x2 35.4 us: on_device(): rho = jnp.take(densities, classes)]
  transfers between devices with their start and end apart: 12 -> 0, of which waited for: 8 -> 0; matrix products, arithmetic and copies ran while one was open for 0% -> 0% of each run, Pallas kernels for 0% -> 0%
where the time goes in v1:
time: 61.2 us; the launch traced here: 61 us
  Pallas kernels  56 us (92%)
  local copies, waits for them, and re-layouts  4.31 us (7%)
  between operations  0.65 us (1%)
    pallas_call x1, Pallas kernels, on_device(): pl.pallas_call(functools.partial(kernel, shape), out_shape=(out, out, out...  56 us
    unnamed x7, local copies, waits for them, and re-layouts  3.15 us

profile of v1, /device:TPU:1, one launch (start us, length us, event | category | flops | bytes accessed | tf_op | source)
XLA Modules:
  0.0 61.0 jit_solution(7407826592616595609)
XLA Ops:
  0.6 1.2 %pad_bitcast_fusion.densities_hbm = f32[1,128]{1,0:T(1,128)} fusion(f32[64]{0:T(128)} %param.5), kind=kLoop, calls=%fused_computation | loop fusion | bytes 768 | tf_op jit(solution)/shard_map/reshape | solution.py:524
  1.8 56.0 %step.1 = (f32[3,8,8,128]{3,2,1,0:T(8,128)}, f32[3,8,8,128]{3,2,1,0:T(8,128)}, f32[3,8,8,128]{3,2,1,0:T(8,128)}) custom-call(f32[3,8,8,128]{3,2,1,0:T(8,128)} %load_hbm.1, s32[7,7,127]{2,1,0:T(8,128)} %classes_hbm.1, f32[1,128]{1,0:T(1,128)} %pad_bitcast_fusion.densities_hbm), custom_call_target="tpu_custom_call" | custom-call | tf_op jit(solution)/shard_map/step/pallas_call | solution.py:526
  57.8 0.0 copy-start.1
  57.8 1.6 %copy.9 = f32[3,8,8,128]{3,2,1,0:T(8,128)} copy(f32[3,8,8,128]{3,2,1,0:T(8,128)} %get-tuple-element.6) | data formatting | bytes 196608
  59.4 0.0 copy-done.1
  59.4 0.0 copy-start
  59.4 0.6 %copy.10 = f32[3,8,8,128]{3,2,1,0:T(8,128)} copy(f32[3,8,8,128]{3,2,1,0:T(8,128)S(1)} %copy-done.1) | data formatting | bytes 196608
  60.0 0.3 copy-done
  60.3 0.6 %copy.11 = f32[3,8,8,128]{3,2,1,0:T(8,128)} copy(f32[3,8,8,128]{3,2,1,0:T(8,128)S(1)} %copy-done) | data formatting | bytes 196608
Async XLA Ops:
  57.8 1.6 %copy-start.1 = (f32[3,8,8,128]{3,2,1,0:T(8,128)S(1)}, f32[3,8,8,128]{3,2,1,0:T(8,128)}, u32[]{:S(2)}) copy-start(f32[3,8,8,128]{3,2,1,0:T(8,128)} %get-tuple-element.7) | copy-start | bytes 294916
  59.4 0.9 %copy-start = (f32[3,8,8,128]{3,2,1,0:T(8,128)S(1)}, f32[3,8,8,128]{3,2,1,0:T(8,128)}, u32[]{:S(2)}) copy-start(f32[3,8,8,128]{3,2,1,0:T(8,128)} %get-tuple-element.8) | copy-start | bytes 294916

commit v2 on v1

v2 whole, which is shorter than its diff:
```python
import functools
import math

import jax
import jax.numpy as jnp
import numpy as np
from jax import lax
from jax.experimental import pallas as pl
from jax.experimental.pallas import tpu as pltpu
from jax.sharding import PartitionSpec as P

MESH = pl.DeviceIdType.MESH
soft_floor = 0.001
poisson = 0.3
lame = poisson / ((1.0 + poisson) * (1.0 - 2.0 * poisson))
shear = 0.5 / (1.0 + poisson)

MASS = (0.25, 1.0 / 12.0)
MODES = [(mx, my, mz) for mx in (0, 1) for my in (0, 1) for mz in (0, 1)]


def mode_couplings():
    rows = {(c, m): [] for c in range(3) for m in MODES}
    for c in range(3):
        for m in MODES:
            own = 0.0
            for axis in range(3):
                if m[axis] == 1:
                    factor = lame + 2.0 * shear if axis == c else shear
                    others = [MASS[m[o]] for o in range(3) if o != axis]
                    own += factor * others[0] * others[1]
            if own:
                rows[c, m].append((own, c, m))
            for k in range(3):
                if k == c:
                    continue
                rest = 3 - c - k
                if m[c] == 1 and m[k] == 0:
                    factor = lame
                elif m[c] == 0 and m[k] == 1:
                    factor = shear
                else:
                    continue
                partner = list(m)
                partner[c], partner[k] = m[k], m[c]
                rows[c, m].append((factor * 0.25 * MASS[m[rest]], k, tuple(partner)))
    return rows


COUPLINGS = mode_couplings()
CORNER_DIAGONAL = sum(w for m in MODES for w, c, _ in COUPLINGS[0, m] if c == 0)


def apply_modes(u, s):
    out = {}
    for c in range(3):
        for m in MODES:
            total = None
            for weight, k, partner in COUPLINGS[c, m]:
                term = u[(k,) + partner] * weight
                total = term if total is None else total + term
            out[(c,) + m] = None if total is None else total * s
    return out


def roll(v, shift, axis):
    return pltpu.roll(v, shift % v.shape[axis], axis)


def inverse(d):
    return 1.0 / jnp.where(d > 0.0, d * CORNER_DIAGONAL, 1.0)


def wide(tile):
    return jnp.broadcast_to(tile, (8, 128))


def total_of(tile):
    return jnp.sum(jnp.sum(tile, axis=0, keepdims=True), axis=1, keepdims=True)


def strip_sums(lower, upper, counted):
    lane = lax.broadcasted_iota(jnp.int32, (16, 128), 1)
    first = lane < 64
    place = lax.rem(lane, 64)
    column, layer = lax.rem(place, 3), lax.div(place, 3)

    def shared(v):
        joined = v + jnp.where(first, roll(v, -62, 1), roll(v, 62, 1))
        return jnp.where(column == jnp.where(first, 2, 0), joined, v)

    def field(f):
        return jnp.where(first, roll(lower, -27 * f, 1), roll(upper, 61 - 27 * f, 1))

    s = jnp.zeros((16, 128), jnp.float32)
    row = lax.broadcasted_iota(jnp.int32, (16, 128), 0)
    for z in range(8):
        found = jnp.where(first, roll(lower, z - 108, 1), roll(upper, z - 111 + 64, 1))
        s = jnp.where(jnp.logical_and(layer == z, column < 2), found, s)
    s = jnp.where(row < 8, s, 0.0)
    d = shared(field(3))
    inv = inverse(d)
    starts, vectors, u = [], [], {}
    for c in range(3):
        start = shared(field(c))
        p = start * inv
        starts.append(start)
        vectors.append(p)
        q = roll(p, -1, 1)
        for mx, along_x in enumerate((p + q, q - p)):
            q = roll(along_x, -1, 0)
            for my, along_y in enumerate((along_x + q, q - along_x)):
                q = roll(along_y, -3, 1)
                u[c, mx, my, 0] = along_y + q
                u[c, mx, my, 1] = q - along_y
    f = apply_modes(u, s)
    rz = curvature = square = jnp.zeros((16, 128), jnp.float32)
    parts = []

    def back(a, b, shift, axis):
        low, high = (-b, b) if a is None else (a - b, a + b)
        return low + roll(high, shift, axis)

    for c in range(3):
        x_parts = []
        for mx in range(2):
            y_parts = [back(f[c, mx, my, 0], f[c, mx, my, 1], 3, 1) for my in range(2)]
            x_parts.append(back(y_parts[0], y_parts[1], 1, 0))
        image = shared(back(x_parts[0], x_parts[1], 1, 1))
        scaled = image * inv
        rz = rz + jnp.where(counted, starts[c] * vectors[c], 0.0)
        curvature = curvature + jnp.where(counted, vectors[c] * image, 0.0)
        square = square + jnp.where(counted, image * scaled, 0.0)
        moved = jnp.where(first, roll(starts[c], -2, 1), roll(starts[c], 2, 1))
        parts.append(jnp.where(column == jnp.where(first, 0, 2), moved, image)[0:8])
    parts.append(d[0:8])
    lane8 = lane[0:8]
    for_lower = for_upper = jnp.zeros((8, 128), jnp.float32)
    for i, part in enumerate(parts):
        here = lax.div(lane8, 24) == i
        for_lower = jnp.where(here, roll(part, 24 * i, 1), for_lower)
        for_upper = jnp.where(here, roll(part, 24 * i - 64, 1), for_upper)
    return (rz, curvature, square), for_lower, for_upper


def kernel(
    shape,
    load_hbm, classes_hbm, densities_hbm,
    displacement_ref, residual_ref, direction_ref,
    load_v, classes_v, table_v, cells_v,
    S, ZL, ZU, YH, YLO, YL, YU, CLL, CLU, CUL, CUU,
    A, G, SL, SU, SR, XM, IM, INV, FZ, FYS, FY, FYZ, RS, LOW, HIGH,
    RA, RB, rows_v,
    in_sem, y_send, y_recv, x_send, x_recv, f_send, f_recv, a_send, a_recv, relay,
):
    NGX, NGY, NGZ = shape
    ring = NGX // 2 * NGZ
    gx, gy, gz = (lax.axis_index(a) for a in ("gx", "gy", "gz"))
    core = lax.rem(gx, 2)
    along = lax.div(gx, 2) * NGZ + gz
    pivot = NGX - 2
    mirrored = gx >= pivot
    has_face = jnp.logical_or(jnp.logical_and(mirrored, gx > 0), gx < pivot - 1)
    gives_left = jnp.logical_and(gx >= 1, gx <= pivot - 1)
    gives_right = jnp.logical_and(gx >= pivot - 1, gx <= NGX - 2)

    def both(dy, dz):
        terms = []
        if dy:
            terms.append(gy > 0 if dy < 0 else gy < NGY - 1)
        if dz:
            terms.append(gz > 0 if dz < 0 else gz < NGZ - 1)
        return terms[0] if len(terms) == 1 else jnp.logical_and(terms[0], terms[1])

    def ring_device(offset, flip=False):
        q = lax.rem(along + (offset % ring), ring)
        c = 1 - core if flip else core
        return {"gx": lax.div(q, NGZ) * 2 + c, "gy": gy, "gz": lax.rem(q, NGZ)}

    def row_device(offset, flip=False):
        c = 1 - core if flip else core
        return {"gx": gx - core + c, "gy": lax.rem(gy + offset, NGY), "gz": gz}

    def plane_device(dy, dx):
        y, x = lax.rem(lax.div(gy, 4) + dy, 4), lax.rem(lax.rem(gy, 4) + dx, 4)
        return {"gx": gx, "gy": y * 4 + x, "gz": gz}

    def block_device(dx, dy, dz):
        return {"gx": gx + dx, "gy": gy + dy, "gz": gz + dz}

    sides = [(dy, dz) for dy in (-1, 0, 1) for dz in (-1, 0, 1) if (dy, dz) != (0, 0)]
    side_buffer = {
        (0, -1): ZL, (0, 1): ZU, (-1, 0): YL, (1, 0): YU,
        (-1, -1): CLL, (-1, 1): CLU, (1, -1): CUL, (1, 1): CUU,
    }

    for (dy, dz), buffer in side_buffer.items():
        @pl.when(jnp.logical_not(both(dy, dz)))
        def _(buffer=buffer):
            buffer[...] = jnp.zeros_like(buffer)
    SR[...] = jnp.zeros_like(SR)

    barrier = pltpu.get_barrier_semaphore()

    def tell(device, semaphore):
        pl.semaphore_signal(semaphore, inc=1, device_id=device, device_id_type=MESH)

    near = [ring_device(o) for o in sorted({1, 2, ring - 1, ring - 2})]
    if NGY == 16:
        plane = [plane_device(*o) for o in ((0, 1), (0, 3), (1, 0), (3, 0))]
        plane_far = [plane_device(*o) for o in ((0, 2), (2, 0))]
    else:
        plane, plane_far = [row_device(o) for o in range(1, NGY)], []
    flipped = row_device(0, True)
    relays = [
        ([ring_device(o) for o in (2, -2)] if ring >= 8 else []) + plane,
        ([ring_device(o) for o in (4, -4)] if ring >= 16 else []) + plane_far,
        [flipped],
        [ring_device(o) for o in (8, -8)] if ring >= 32 else [],
    ]

    def relay_tell(step):
        for device in relays[step]:
            tell(device, relay.at[step])

    def relay_wait(step):
        if relays[step]:
            pl.semaphore_wait(relay.at[step], len(relays[step]))

    awaited = jnp.int32(0)
    for dy, dz in sorted(sides, key=lambda side: -abs(side[0]) - abs(side[1])):
        @pl.when(both(dy, dz))
        def _(dy=dy, dz=dz):
            tell(block_device(0, dy, dz), barrier)
        awaited = awaited + both(dy, dz).astype(jnp.int32)
    for device in near + plane + [flipped]:
        tell(device, barrier)
        awaited = awaited + 1

    @pl.when(jnp.logical_and(gx < pivot - 1, core == 1))
    def _():
        tell(block_device(1, 0, 0), barrier)
    awaited = awaited + jnp.logical_and(gives_left, core == 0).astype(jnp.int32)

    loads = [
        pltpu.make_async_copy(classes_hbm, classes_v, in_sem.at[0]),
        pltpu.make_async_copy(densities_hbm, table_v, in_sem.at[1]),
        pltpu.make_async_copy(load_hbm, load_v, in_sem.at[2]),
    ]
    for copy in loads:
        copy.start()

    lane = lax.broadcasted_iota(jnp.int32, (8, 128), 1)
    sub = lax.broadcasted_iota(jnp.int32, (8, 128), 0)
    lane1 = lax.broadcasted_iota(jnp.int32, (1, 128), 1)
    third, third1 = lax.div(lane, 3), lax.div(lane1, 3)

    cells_v[...] = jnp.zeros_like(cells_v)
    loads[0].wait()
    cells_v[:, 0:7, 0:127] = classes_v[...]
    loads[1].wait()
    rho = table_v[...]
    rho = jnp.concatenate([rho, rho], axis=1)
    table = wide(soft_floor + rho * rho * rho * (1.0 - soft_floor))
    inside = jnp.logical_and(sub < 7, lane < 127)
    previous = jnp.zeros((8, 128), jnp.float32)
    for z in range(8):
        if z < 7:
            picked = jnp.take_along_axis(table, cells_v[z], axis=1, mode="promise_in_bounds")
            s = jnp.where(inside, picked, 0.0)
        else:
            s = jnp.zeros((8, 128), jnp.float32)
        S[z, 4] = s
        s = s + roll(s, 1, 1)
        s = s + roll(s, 1, 0)
        S[z, 3] = s + previous
        previous = s
    loads[2].wait()
    for z in range(8):
        for c in range(3):
            S[z, c] = load_v[c, z]
    for f in range(4):
        YH[f] = jnp.concatenate([S[z, f, 7:8, :] for z in range(8)], axis=0)
        YLO[f] = jnp.concatenate([S[z, f, 0:1, :] for z in range(8)], axis=0)
        YLO[4 + f] = jnp.concatenate([S[z, f, 1:2, :] for z in range(8)], axis=0)
    YLO[8] = jnp.concatenate([S[z, 4, 0:1, :] for z in range(8)], axis=0)

    pl.semaphore_wait(barrier, awaited)

    def remote(source, target, sends, recvs, index, device):
        return pltpu.make_async_remote_copy(
            src_ref=source, dst_ref=target, send_sem=sends.at[index], recv_sem=recvs.at[index],
            device_id=device, device_id_type=MESH,
        )

    source_of = {
        (0, -1): S.at[pl.ds(0, 2)],
        (0, 1): S.at[7, pl.ds(0, 4)],
        (-1, 0): YLO,
        (1, 0): YH,
        (-1, -1): YLO.at[:, pl.ds(0, 2)],
        (-1, 1): YLO.at[pl.ds(0, 8), pl.ds(7, 1)],
        (1, -1): YH.at[:, pl.ds(0, 2)],
        (1, 1): YH.at[:, pl.ds(7, 1)],
    }
    y_copies = {
        (dy, dz): remote(source_of[dy, dz], side_buffer[-dy, -dz], y_send, y_recv, sides.index((dy, dz)), block_device(0, dy, dz))
        for dy, dz in sides
    }
    for dy, dz in sorted(sides, key=lambda side: -abs(side[0]) - abs(side[1])):
        @pl.when(both(dy, dz))
        def _(copy=y_copies[dy, dz]):
            copy.start()
    relay_tell(0)
    relay_wait(0)
    relay_tell(1)
    for dy, dz in sides:
        @pl.when(both(dy, dz))
        def _(copy=y_copies[-dy, -dz]):
            copy.wait_recv()

    top, bottom = sub == 0, sub == 7
    for f in range(4):
        low = YL[f] + jnp.where(top, wide(CLL[f]), 0.0) + jnp.where(bottom, wide(CLU[f, 0:1]), 0.0)
        low8 = CLU[f, 1:2]
        high = YU[f] + jnp.where(top, wide(CUL[f]), 0.0) + jnp.where(bottom, wide(CUU[f, 0:1]), 0.0)
        high8 = CUU[f, 1:2]
        G[f, 0:8] = YU[4 + f] + jnp.where(top, wide(CUL[4 + f]), 0.0) + jnp.where(bottom, wide(CUU[4 + f, 0:1]), 0.0)
        G[f, 8:9] = CUU[4 + f, 1:2]
        for z in range(9):
            tile = S[z, f] if z < 8 else ZU[1, f]
            if z == 0:
                tile = tile + ZL[f]
            if z == 7:
                tile = tile + ZU[0, f]
            lower = low[z : z + 1] if z < 8 else low8
            upper = high[z : z + 1] if z < 8 else high8
            A[z, f] = tile + jnp.where(top, wide(lower), 0.0) + jnp.where(bottom, wide(upper), 0.0)
    edge = YU[8]
    for z in range(8):
        tile = S[z, 4] if z < 7 else ZU[0, 4]
        row = edge[z : z + 1] if z < 7 else CUU[8, 0:1]
        A[z, 4] = jnp.where(bottom, wide(row), tile)

    low_tile = high_tile = jnp.zeros((8, 128), jnp.float32)
    low_row = high_row = jnp.zeros((1, 128), jnp.float32)
    for f in range(4):
        for z in range(9):
            k = 9 * f + z
            tile = roll(A[z, f], 3 * k - 125, 1)
            high_tile = jnp.where(third == k, tile, high_tile)
            low_tile = jnp.where(third == k + 1, tile, low_tile)
            row = roll(G[f, z : z + 1], 3 * k - 125, 1)
            high_row = jnp.where(third1 == k, row, high_row)
            low_row = jnp.where(third1 == k + 1, row, low_row)
    for z in range(8):
        tile = roll(A[z, 4], 108 + 2 * z - 125, 1)
        high_tile = jnp.where(lax.div(lane - 108, 2) == z if z else jnp.logical_or(lane == 108, lane == 109), tile, high_tile)
        low_tile = jnp.where(lax.div(lane - 111, 2) == z if z else jnp.logical_or(lane == 111, lane == 112), tile, low_tile)
    for buffer, tile, row in ((SL, high_tile, high_row), (SU, low_tile, low_row)):
        buffer[0:8] = tile
        buffer[8:9] = row
        buffer[9:16] = jnp.zeros((7, 128), jnp.float32)

    nine = pl.ds(0, 9)
    to_left = remote(SU.at[nine], SR.at[nine], x_send, x_recv, 0, block_device(-1, 0, 0))
    to_right = remote(SL.at[nine], SR.at[nine], x_send, x_recv, 1, block_device(1, 0, 0))

    @pl.when(gives_left)
    def _():
        to_left.start()

    relay_wait(1)
    relay_tell(2)
    relay_wait(2)

    @pl.when(gives_right)
    def _():
        to_right.start()

    relay_tell(3)

    keep = jnp.logical_or(lane > 0, gx > 0)
    keep1 = jnp.logical_or(lane1 > 0, gx > 0)
    inv_side = inverse(G[3, 0:8])
    inv_corner = inverse(G[3, 8:9])

    def along_x(p):
        q = roll(p, -1, 1)
        return p + q, q - p

    side = [along_x(jnp.where(keep, G[c, 0:8], 0.0) * inv_side) for c in range(3)]
    corner = [along_x(jnp.where(keep1, G[c, 8:9], 0.0) * inv_corner) for c in range(3)]
    owned = jnp.logical_and(
        jnp.logical_and(jnp.logical_or(lane > 1, gx == 0), jnp.logical_or(lane < 126, gx == NGX - 1)),
        jnp.logical_or(sub > 0, gy == 0),
    )
    owned_first = jnp.logical_and(owned, gz == 0)
    rz = jnp.zeros((8, 128), jnp.float32)
    for z in range(9):
        inv = inverse(A[z, 3])
        INV[z] = inv
        for c in range(3):
            start = jnp.where(keep, A[z, c], 0.0)
            p = start * inv
            if z < 8:
                A[z, c] = start
                rz = rz + jnp.where(owned if z else owned_first, start * p, 0.0)
            sums = along_x(p)
            for m in range(2):
                XM[z, c, m, 0:8] = sums[m]
                XM[z, c, m, 8:9] = side[c][m][z : z + 1] if z < 8 else corner[c][m]

    def plane_modes(z):
        modes = {}
        for c in range(3):
            for mx in range(2):
                here, above = XM[z, c, mx, 0:8], XM[z, c, mx, 1:9]
                modes[c, mx, 0] = here + above
                modes[c, mx, 1] = above - here
        return modes

    def spread(first, second, axis, mask):
        return first - second + jnp.where(mask, roll(first + second, 1, axis), 0.0)

    curvature = jnp.zeros((8, 128), jnp.float32)
    square = jnp.zeros((8, 128), jnp.float32)
    lower = plane_modes(0)
    carried = None
    for z in range(8):
        upper = plane_modes(z + 1)
        u = {}
        for key in lower:
            u[key + (0,)] = lower[key] + upper[key]
            u[key + (1,)] = upper[key] - lower[key]
        f = apply_modes(u, A[z, 4])
        here, carry = {}, {}
        for c in range(3):
            for mx in range(2):
                for my in range(2):
                    first, second = f[c, mx, my, 0], f[c, mx, my, 1]
                    if first is None:
                        here[c, mx, my], carry[c, mx, my] = -second, second
                    else:
                        here[c, mx, my], carry[c, mx, my] = first - second, first + second
        if carried is not None:
            here = {key: here[key] + carried[key] for key in here}
        carried = carry
        lower = upper
        inv = INV[z]
        mask = owned if z else owned_first
        for c in range(3):
            rows = [spread(here[c, mx, 0], here[c, mx, 1], 0, sub > 0) for mx in range(2)]
            image = jnp.where(keep, spread(rows[0], rows[1], 1, lane > 0), 0.0)
            IM[z, c] = image
            scaled = image * inv
            curvature = curvature + jnp.where(mask, A[z, c] * scaled, 0.0)
            square = square + jnp.where(mask, image * scaled, 0.0)

    @pl.when(jnp.logical_and(has_face, jnp.logical_not(mirrored)))
    def _():
        to_left.wait_recv()

    @pl.when(jnp.logical_and(has_face, mirrored))
    def _():
        to_right.wait_recv()

    lane16 = lax.broadcasted_iota(jnp.int32, (16, 128), 1)
    sub16 = lax.broadcasted_iota(jnp.int32, (16, 128), 0)
    place = lax.rem(lane16, 64)
    column, layer = lax.rem(place, 3), lax.div(place, 3)
    counted = jnp.logical_and(
        jnp.logical_and(
            jnp.logical_and(sub16 < 8, jnp.logical_or(sub16 > 0, gy == 0)),
            jnp.logical_and(layer < 8, jnp.logical_or(layer > 0, gz == 0)),
        ),
        jnp.logical_and(has_face, jnp.where(lane16 < 64, column, 2 - 2 * jnp.abs(column - 1)) > 0),
    )
    received = SR[...]
    sums, for_lower, for_upper = strip_sums(
        jnp.where(mirrored, received, SL[...]), jnp.where(mirrored, SU[...], received), counted
    )
    rz, curvature, square = (
        total_of(own + part[0:8] + part[8:16]) for own, part in zip((rz, curvature, square), sums)
    )

    row = jnp.where(lane1 == 0, rz, jnp.where(lane1 == 1, curvature, square))
    rows_v[0:1] = row
    RA[0:1] = row
    for flip in (True, False):
        for k in range(NGY):
            if k or flip:
                slot = k + (NGY if flip else 0)
                remote(rows_v.at[pl.ds(0, 1)], RA.at[pl.ds(slot, 1)], a_send, a_recv, 0, row_device(k, flip)).start()

    RS[0] = for_lower
    RS[1] = for_upper
    result_right = remote(RS.at[1], LOW, f_send, f_recv, 3, block_device(1, 0, 0))
    result_left = remote(RS.at[0], HIGH, f_send, f_recv, 4, block_device(-1, 0, 0))
    normal_face = jnp.logical_and(has_face, jnp.logical_not(mirrored))
    mirrored_face = jnp.logical_and(has_face, mirrored)

    @pl.when(normal_face)
    def _():
        result_right.start()
        HIGH[...] = for_lower

    @pl.when(mirrored_face)
    def _():
        result_left.start()
        LOW[...] = for_upper

    def drain(ref, count, semaphore):
        block = ref.at[pl.ds(0, count)]
        pltpu.make_async_copy(block, block, semaphore).wait()

    drain(RA, 2 * NGY - 1, a_recv.at[0])
    row = jnp.sum(RA[...], axis=0, keepdims=True)
    rows_v[1:2] = row
    RB[0:1] = row
    relay_wait(3)
    for k in sorted(range(1, ring), key=lambda k: -min(k, ring - k)):
        remote(rows_v.at[pl.ds(1, 1)], RB.at[pl.ds(k, 1)], a_send, a_recv, 1, ring_device(k)).start()

    @pl.when(gives_left)
    def _():
        result_right.wait_recv()

    @pl.when(jnp.logical_or(gives_left, mirrored_face))
    def _():
        tile = LOW[...]
        for z in range(8):
            diagonal = roll(tile, -(72 + 3 * z), 1)
            INV[z] = jnp.where(lane == 0, inverse(diagonal), INV[z])
            for c in range(3):
                k = 24 * c + 3 * z
                IM[z, c] = jnp.where(lane < 2, roll(tile, -k, 1), IM[z, c])
                A[z, c] = jnp.where(lane == 0, roll(tile, -(k + 2), 1), A[z, c])

    @pl.when(gives_right)
    def _():
        result_left.wait_recv()

    @pl.when(jnp.logical_or(gives_right, normal_face))
    def _():
        tile = HIGH[...]
        for z in range(8):
            diagonal = roll(tile, 127 - (72 + 3 * z + 2), 1)
            INV[z] = jnp.where(lane == 127, inverse(diagonal), INV[z])
            for c in range(3):
                k = 24 * c + 3 * z
                IM[z, c] = jnp.where(lane > 125, roll(tile, 127 - (k + 2), 1), IM[z, c])
                A[z, c] = jnp.where(lane == 127, roll(tile, 127 - k, 1), A[z, c])

    for c in range(3):
        FYS[c] = jnp.concatenate([IM[z, c, 7:8, :] for z in range(8)], axis=0)
    z_fix = remote(IM.at[7], FZ, f_send, f_recv, 0, block_device(0, 0, 1))
    y_fix = remote(FYS, FY, f_send, f_recv, 1, block_device(0, 1, 0))
    yz_fix = remote(FYS.at[:, pl.ds(7, 1)], FYZ, f_send, f_recv, 2, block_device(0, 1, 1))
    fixes = ((yz_fix, 1, 1), (y_fix, 1, 0), (z_fix, 0, 1))
    for copy, dy, dz in fixes:
        @pl.when(both(dy, dz))
        def _(copy=copy):
            copy.start()
    for dy, dz in sides:
        @pl.when(both(dy, dz))
        def _(copy=y_copies[dy, dz]):
            copy.wait_send()
    for copy, dy, dz in fixes:
        @pl.when(both(-dy, -dz))
        def _(copy=copy):
            copy.wait_recv()
    for copy, dy, dz in fixes:
        @pl.when(both(dy, dz))
        def _(copy=copy):
            copy.wait_send()

    @pl.when(gz > 0)
    def _():
        IM[0] = FZ[...]

    @pl.when(gy > 0)
    def _():
        for c in range(3):
            for z in range(8):
                IM[z, c, 0:1, :] = FY[c, z : z + 1, :]

    @pl.when(both(-1, -1))
    def _():
        for c in range(3):
            IM[0, c, 0:1, :] = FYZ[c]

    for copy, condition in (
        (to_left, gives_left), (to_right, gives_right), (result_right, normal_face), (result_left, mirrored_face),
    ):
        @pl.when(condition)
        def _(copy=copy):
            copy.wait_send()
    drain(RA, 2 * NGY - 1, a_send.at[0])
    drain(RB, ring - 1, a_recv.at[1])
    row = jnp.sum(RB[...], axis=0, keepdims=True)
    rz, curvature, square = (row[:, i : i + 1] for i in range(3))
    alpha = rz / curvature
    beta = alpha * alpha * square / rz - 1.0
    alpha, beta = wide(alpha), wide(beta)
    for z in range(8):
        inv = INV[z]
        for c in range(3):
            start = A[z, c]
            p = start * inv
            residual = start - alpha * IM[z, c]
            displacement_ref[c, z] = alpha * p
            residual_ref[c, z] = residual
            direction_ref[c, z] = residual * inv + beta * p
    drain(RB, ring - 1, a_send.at[1])


def store_kernel(a_ref, b_ref, c_ref, a_out, b_out, c_out, sem):
    copies = [
        pltpu.make_async_copy(source, target, sem.at[i])
        for i, (source, target) in enumerate(((a_ref, a_out), (b_ref, b_out), (c_ref, c_out)))
    ]
    for copy in copies:
        copy.start()
    for copy in copies:
        copy.wait()


def on_device(shape, load, classes, densities):
    f32, i32 = jnp.float32, jnp.int32
    ring = shape[0] // 2 * shape[2]
    dma = pltpu.SemaphoreType.DMA

    def rows(n):
        return pltpu.VMEM((n, 128), f32)

    def tiles(*dims):
        return pltpu.VMEM(dims + (8, 128), f32)

    out = jax.ShapeDtypeStruct(load.shape, f32)
    outs = pl.pallas_call(
        functools.partial(kernel, shape),
        out_shape=(out, out, out),
        in_specs=[pl.BlockSpec(memory_space=pl.ANY)] * 3,
        out_specs=(pl.BlockSpec(memory_space=pltpu.VMEM),) * 3,
        scratch_shapes=[
            pltpu.VMEM(load.shape, f32), pltpu.VMEM(classes.shape, i32), pltpu.VMEM((1, 64), f32), pltpu.VMEM((7, 8, 128), i32),
            tiles(8, 5), tiles(4), tiles(2, 5), tiles(4), tiles(9), tiles(4), tiles(9),
            pltpu.VMEM((4, 1, 128), f32), pltpu.VMEM((4, 2, 128), f32), pltpu.VMEM((8, 1, 128), f32), pltpu.VMEM((9, 2, 128), f32),
            tiles(9, 5), pltpu.VMEM((4, 16, 128), f32), rows(16), rows(16), rows(16),
            pltpu.VMEM((9, 3, 2, 16, 128), f32), tiles(8, 3), tiles(9),
            tiles(3), tiles(3), tiles(3), pltpu.VMEM((3, 1, 128), f32), tiles(2), tiles(), tiles(),
            rows(2 * shape[1]), rows(ring), rows(2),
            dma((3,)), dma((8,)), dma((8,)), dma((2,)), dma((2,)), dma((5,)), dma((5,)), dma((2,)), dma((2,)),
            pltpu.SemaphoreType.REGULAR((4,)),
        ],
        compiler_params=pltpu.CompilerParams(collective_id=0, has_side_effects=True),
        name="step",
    )(load, classes, densities.reshape(1, 64))
    return pl.pallas_call(
        store_kernel,
        out_shape=(out, out, out),
        in_specs=[pl.BlockSpec(memory_space=pltpu.VMEM)] * 3,
        out_specs=(pl.BlockSpec(memory_space=pl.ANY),) * 3,
        scratch_shapes=[dma((3,))],
        name="store",
    )(*outs)


def solution(mesh):
    shape = tuple(mesh.shape[a] for a in ("gx", "gy", "gz"))
    spec = P(None, "gz", "gy", "gx")
    return jax.shard_map(
        functools.partial(on_device, shape), mesh=mesh,
        in_specs=(spec, P("gz", "gy", "gx"), P()), out_specs=(spec, spec, spec), check_vma=False,
    )
```

time: 61.2 us -> 52.9 us (0.86)
  local copies, waits for them, and re-layouts: 4.31 us -> 0 us
  Pallas kernels: 56 us -> 52.1 us
    pallas_call x1, Pallas kernels: 56 us -> 50.4 us  [on_device(): pl.pallas_call(functools.partial(kernel, shape), out_shape=(out, out, out...]
    unnamed x7 -> x0, local copies, waits for them, and re-layouts: 3.15 us -> none
    pallas_call x0 -> x1, Pallas kernels: none -> 1.72 us  [on_device(): pl.pallas_call(store_kernel, out_shape=(out, out, out), in_specs=[pl.Bloc...]
    reshape x1 -> x0, local copies, waits for them, and re-layouts: 1.17 us -> none  [on_device(): table = jnp.pad(densities, (0, 64)).reshape(1, 128)]
where the time goes in v2:
time: 52.9 us; the launch traced here: 52.7 us
  Pallas kernels  52.1 us (98%)
  between operations  0.64 us (1%)
    pallas_call x1, Pallas kernels, on_device(): pl.pallas_call(functools.partial(kernel, shape), out_shape=(out, out, out...  50.4 us
    pallas_call x1, Pallas kernels, on_device(): pl.pallas_call(store_kernel, out_shape=(out, out, out), in_specs=[pl.Bloc...  1.72 us

profile of v2, /device:TPU:1, one launch (start us, length us, event | category | flops | bytes accessed | tf_op | source)
XLA Modules:
  0.0 52.7 jit_solution(951975503135316978)
XLA Ops:
  0.6 50.4 %step.1 = (f32[3,8,8,128]{3,2,1,0:T(8,128)}, f32[3,8,8,128]{3,2,1,0:T(8,128)}, f32[3,8,8,128]{3,2,1,0:T(8,128)}) custom-call(f32[3,8,8,128]{3,2,1,0:T(8,128)} %load_hbm.1, s32[7,7,127]{2,1,0:T(8,128)} %classes_hbm.1, f32[1,64]{1,0:T(1,128)} %bitcast.1), custom_call_target="tpu_custom_call" | custom-call | tf_op jit(solution)/shard_map/step/pallas_call | solution.py:641
  51.0 1.7 %store.1 = (f32[3,8,8,128]{3,2,1,0:T(8,128)}, f32[3,8,8,128]{3,2,1,0:T(8,128)}, f32[3,8,8,128]{3,2,1,0:T(8,128)}) custom-call(f32[3,8,8,128]{3,2,1,0:T(8,128)} %get-tuple-element.6.a_ref, f32[3,8,8,128]{3,2,1,0:T(8,128)} %get-tuple-element.7.b_ref, f32[3,8,8,128]{3,2,1,0:T(8,128)} %get-tuple-element.8.c_ref), custom_call_target="tpu_custom_call" | custom-call | tf_op jit(solution)/shard_map/store/pallas_call | solution.py:660

commit v3 on v2

--- a/solution.py
+++ b/solution.py
@@ -158,7 +158,7 @@
     gx, gy, gz = (lax.axis_index(a) for a in ("gx", "gy", "gz"))
     core = lax.rem(gx, 2)
     along = lax.div(gx, 2) * NGZ + gz
-    pivot = NGX - 2
+    pivot = jnp.where(gz < 5 * NGZ // 8, NGX - 2, NGX - 4)
     mirrored = gx >= pivot
     has_face = jnp.logical_or(jnp.logical_and(mirrored, gx > 0), gx < pivot - 1)
     gives_left = jnp.logical_and(gx >= 1, gx <= pivot - 1)
@@ -181,9 +181,10 @@
         c = 1 - core if flip else core
         return {"gx": gx - core + c, "gy": lax.rem(gy + offset, NGY), "gz": gz}
 
-    def plane_device(dy, dx):
+    def plane_device(dy, dx, flip=False):
         y, x = lax.rem(lax.div(gy, 4) + dy, 4), lax.rem(lax.rem(gy, 4) + dx, 4)
-        return {"gx": gx, "gy": y * 4 + x, "gz": gz}
+        c = 1 - core if flip else core
+        return {"gx": gx - core + c, "gy": y * 4 + x, "gz": gz}
 
     def block_device(dx, dy, dz):
         return {"gx": gx + dx, "gy": gy + dy, "gz": gz + dz}
@@ -227,7 +228,11 @@
         if relays[step]:
             pl.semaphore_wait(relay.at[step], len(relays[step]))
 
-    awaited = jnp.int32(0)
+    @pl.when(jnp.logical_and(gx < pivot - 1, core == 1))
+    def _():
+        tell(block_device(1, 0, 0), barrier)
+
+    awaited = jnp.logical_and(gives_left, core == 0).astype(jnp.int32)
     for dy, dz in sorted(sides, key=lambda side: -abs(side[0]) - abs(side[1])):
         @pl.when(both(dy, dz))
         def _(dy=dy, dz=dz):
@@ -236,11 +241,6 @@
     for device in near + plane + [flipped]:
         tell(device, barrier)
         awaited = awaited + 1
-
-    @pl.when(jnp.logical_and(gx < pivot - 1, core == 1))
-    def _():
-        tell(block_device(1, 0, 0), barrier)
-    awaited = awaited + jnp.logical_and(gives_left, core == 0).astype(jnp.int32)
 
     loads = [
         pltpu.make_async_copy(classes_hbm, classes_v, in_sem.at[0]),
@@ -370,15 +370,15 @@
     def _():
         to_left.start()
 
-    relay_wait(1)
-    relay_tell(2)
-    relay_wait(2)
+    def relay_far():
+        relay_wait(1)
+        relay_tell(2)
+        relay_wait(2)
 
     @pl.when(gives_right)
     def _():
+        relay_far()
         to_right.start()
-
-    relay_tell(3)
 
     keep = jnp.logical_or(lane > 0, gx > 0)
     keep1 = jnp.logical_or(lane1 > 0, gx > 0)
@@ -456,6 +456,12 @@
             scaled = image * inv
             curvature = curvature + jnp.where(mask, A[z, c] * scaled, 0.0)
             square = square + jnp.where(mask, image * scaled, 0.0)
+
+    @pl.when(jnp.logical_not(gives_right))
+    def _():
+        relay_far()
+
+    relay_tell(3)
 
     @pl.when(jnp.logical_and(has_face, jnp.logical_not(mirrored)))
     def _():
@@ -487,11 +493,15 @@
     row = jnp.where(lane1 == 0, rz, jnp.where(lane1 == 1, curvature, square))
     rows_v[0:1] = row
     RA[0:1] = row
-    for flip in (True, False):
-        for k in range(NGY):
+    def hops(k):
+        return min(k % 4, 4 - k % 4) + min(k // 4, 4 - k // 4)
+
+    for k in sorted(range(NGY), key=lambda k: -hops(k)):
+        for flip in (True, False):
             if k or flip:
+                device = plane_device(k // 4, k % 4, flip) if NGY == 16 else row_device(k, flip)
                 slot = k + (NGY if flip else 0)
-                remote(rows_v.at[pl.ds(0, 1)], RA.at[pl.ds(slot, 1)], a_send, a_recv, 0, row_device(k, flip)).start()
+                remote(rows_v.at[pl.ds(0, 1)], RA.at[pl.ds(slot, 1)], a_send, a_recv, 0, device).start()
 
     RS[0] = for_lower
     RS[1] = for_upper
@@ -641,7 +651,7 @@
     outs = pl.pallas_call(
         functools.partial(kernel, shape),
         out_shape=(out, out, out),
-        in_specs=[pl.BlockSpec(memory_space=pl.ANY)] * 3,
+        in_specs=[pl.BlockSpec(memory_space=pltpu.HBM)] * 3,
         out_specs=(pl.BlockSpec(memory_space=pltpu.VMEM),) * 3,
         scratch_shapes=[
             pltpu.VMEM(load.shape, f32), pltpu.VMEM(classes.shape, i32), pltpu.VMEM((1, 64), f32), pltpu.VMEM((7, 8, 128), i32),
@@ -654,15 +664,16 @@
             dma((3,)), dma((8,)), dma((8,)), dma((2,)), dma((2,)), dma((5,)), dma((5,)), dma((2,)), dma((2,)),
             pltpu.SemaphoreType.REGULAR((4,)),
         ],
-        compiler_params=pltpu.CompilerParams(collective_id=0, has_side_effects=True),
+        compiler_params=pltpu.CompilerParams(collective_id=0, has_side_effects=True, vmem_limit_bytes=8 * 2**20),
         name="step",
-    )(load, classes, densities.reshape(1, 64))
+    )(*(pltpu.with_memory_space_constraint(x, pltpu.HBM) for x in (load, classes, densities.reshape(1, 64))))
     return pl.pallas_call(
         store_kernel,
         out_shape=(out, out, out),
         in_specs=[pl.BlockSpec(memory_space=pltpu.VMEM)] * 3,
         out_specs=(pl.BlockSpec(memory_space=pl.ANY),) * 3,
         scratch_shapes=[dma((3,))],
+        compiler_params=pltpu.CompilerParams(vmem_limit_bytes=2 * 2**20),
         name="store",
     )(*outs)
 

time: 52.9 us -> 50.4 us (0.953)
  Pallas kernels: 52.1 us -> 49.6 us
    pallas_call x1, Pallas kernels: 50.4 us -> 48.9 us  [on_device(): pl.pallas_call(functools.partial(kernel, shape), out_shape=(out, out, out...]
    pallas_call x1, Pallas kernels: 1.72 us -> 0.73 us  [on_device(): pl.pallas_call(store_kernel, out_shape=(out, out, out), in_specs=[pl.Bloc...]
where the time goes in v3:
time: 50.4 us; the launch traced here: 50.3 us
  Pallas kernels  49.6 us (98%)
  between operations  0.64 us (1%)
    pallas_call x1, Pallas kernels, on_device(): pl.pallas_call(functools.partial(kernel, shape), out_shape=(out, out, out...  48.9 us

profile of v3, /device:TPU:1, one launch (start us, length us, event | category | flops | bytes accessed | tf_op | source)
XLA Modules:
  0.0 50.3 jit_solution(5067984223895531999)
XLA Ops:
  0.6 48.9 %step.1 = (f32[3,8,8,128]{3,2,1,0:T(8,128)S(1)}, f32[3,8,8,128]{3,2,1,0:T(8,128)S(1)}, f32[3,8,8,128]{3,2,1,0:T(8,128)S(1)}) custom-call(f32[3,8,8,128]{3,2,1,0:T(8,128)} %load_hbm.1, s32[7,7,127]{2,1,0:T(8,128)} %classes_hbm.1, f32[1,64]{1,0:T(1,128)} %bitcast.1), custom_call_target="tpu_custom_call" | custom-call | tf_op jit(solution)/shard_map/step/pallas_call | solution.py:651
  49.5 0.7 %store.1 = (f32[3,8,8,128]{3,2,1,0:T(8,128)}, f32[3,8,8,128]{3,2,1,0:T(8,128)}, f32[3,8,8,128]{3,2,1,0:T(8,128)}) custom-call(f32[3,8,8,128]{3,2,1,0:T(8,128)S(1)} %get-tuple-element.6.a_ref, f32[3,8,8,128]{3,2,1,0:T(8,128)S(1)} %get-tuple-element.7.b_ref, f32[3,8,8,128]{3,2,1,0:T(8,128)S(1)} %get-tuple-element.8.c_ref), custom_call_target="tpu_custom_call" | custom-call | tf_op jit(solution)/shard_map/store/pallas_call | solution.py:670

commit v4 on v3

--- a/solution.py
+++ b/solution.py
@@ -79,6 +79,14 @@
     return jnp.sum(jnp.sum(tile, axis=0, keepdims=True), axis=1, keepdims=True)
 
 
+def div(a, n):
+    return a >> (n.bit_length() - 1) if n & (n - 1) == 0 else lax.div(a, n)
+
+
+def rem(a, n):
+    return a & (n - 1) if n & (n - 1) == 0 else lax.rem(a, n)
+
+
 def strip_sums(lower, upper, counted):
     lane = lax.broadcasted_iota(jnp.int32, (16, 128), 1)
     first = lane < 64
@@ -156,8 +164,8 @@
     NGX, NGY, NGZ = shape
     ring = NGX // 2 * NGZ
     gx, gy, gz = (lax.axis_index(a) for a in ("gx", "gy", "gz"))
-    core = lax.rem(gx, 2)
-    along = lax.div(gx, 2) * NGZ + gz
+    core = rem(gx, 2)
+    along = div(gx, 2) * NGZ + gz
     pivot = jnp.where(gz < 5 * NGZ // 8, NGX - 2, NGX - 4)
     mirrored = gx >= pivot
     has_face = jnp.logical_or(jnp.logical_and(mirrored, gx > 0), gx < pivot - 1)
@@ -173,16 +181,16 @@
         return terms[0] if len(terms) == 1 else jnp.logical_and(terms[0], terms[1])
 
     def ring_device(offset, flip=False):
-        q = lax.rem(along + (offset % ring), ring)
+        q = rem(along + (offset % ring), ring)
         c = 1 - core if flip else core
-        return {"gx": lax.div(q, NGZ) * 2 + c, "gy": gy, "gz": lax.rem(q, NGZ)}
+        return {"gx": div(q, NGZ) * 2 + c, "gy": gy, "gz": rem(q, NGZ)}
 
     def row_device(offset, flip=False):
         c = 1 - core if flip else core
-        return {"gx": gx - core + c, "gy": lax.rem(gy + offset, NGY), "gz": gz}
+        return {"gx": gx - core + c, "gy": rem(gy + offset, NGY), "gz": gz}
 
     def plane_device(dy, dx, flip=False):
-        y, x = lax.rem(lax.div(gy, 4) + dy, 4), lax.rem(lax.rem(gy, 4) + dx, 4)
+        y, x = rem(div(gy, 4) + dy, 4), rem(rem(gy, 4) + dx, 4)
         c = 1 - core if flip else core
         return {"gx": gx - core + c, "gy": y * 4 + x, "gz": gz}
 
@@ -206,7 +214,7 @@
     def tell(device, semaphore):
         pl.semaphore_signal(semaphore, inc=1, device_id=device, device_id_type=MESH)
 
-    near = [ring_device(o) for o in sorted({1, 2, ring - 1, ring - 2})]
+    near = [ring_device(o, flip) for o in sorted({1, 2, ring - 1, ring - 2}) for flip in (False, True)]
     if NGY == 16:
         plane = [plane_device(*o) for o in ((0, 1), (0, 3), (1, 0), (3, 0))]
         plane_far = [plane_device(*o) for o in ((0, 2), (2, 0))]
@@ -214,8 +222,8 @@
         plane, plane_far = [row_device(o) for o in range(1, NGY)], []
     flipped = row_device(0, True)
     relays = [
-        ([ring_device(o) for o in (2, -2)] if ring >= 8 else []) + plane,
-        ([ring_device(o) for o in (4, -4)] if ring >= 16 else []) + plane_far,
+        ([ring_device(o, flip) for o in (2, -2) for flip in (False, True)] if ring >= 8 else []) + plane,
+        ([ring_device(o, flip) for o in (4, -4) for flip in (False, True)] if ring >= 16 else []) + plane_far,
         [flipped],
         [ring_device(o) for o in (8, -8)] if ring >= 32 else [],
     ]
@@ -370,14 +378,9 @@
     def _():
         to_left.start()
 
-    def relay_far():
+    @pl.when(gives_right)
+    def _():
         relay_wait(1)
-        relay_tell(2)
-        relay_wait(2)
-
-    @pl.when(gives_right)
-    def _():
-        relay_far()
         to_right.start()
 
     keep = jnp.logical_or(lane > 0, gx > 0)
@@ -459,8 +462,10 @@
 
     @pl.when(jnp.logical_not(gives_right))
     def _():
-        relay_far()
-
+        relay_wait(1)
+
+    relay_tell(2)
+    relay_wait(2)
     relay_tell(3)
 
     @pl.when(jnp.logical_and(has_face, jnp.logical_not(mirrored)))
@@ -527,10 +532,12 @@
     drain(RA, 2 * NGY - 1, a_recv.at[0])
     row = jnp.sum(RA[...], axis=0, keepdims=True)
     rows_v[1:2] = row
-    RB[0:1] = row
+    RB[along] = row
     relay_wait(3)
-    for k in sorted(range(1, ring), key=lambda k: -min(k, ring - k)):
-        remote(rows_v.at[pl.ds(1, 1)], RB.at[pl.ds(k, 1)], a_send, a_recv, 1, ring_device(k)).start()
+    for k in range(ring - 1):
+        chip = jnp.where(k < along, k, k + 1)
+        device = {"gx": div(chip, NGZ) * 2 + core, "gy": gy, "gz": rem(chip, NGZ)}
+        remote(rows_v.at[pl.ds(1, 1)], RB.at[along], a_send, a_recv, 1, device).start()
 
     @pl.when(gives_left)
     def _():
@@ -608,7 +615,7 @@
             copy.wait_send()
     drain(RA, 2 * NGY - 1, a_send.at[0])
     drain(RB, ring - 1, a_recv.at[1])
-    row = jnp.sum(RB[...], axis=0, keepdims=True)
+    row = jnp.sum(RB[...], axis=0)
     rz, curvature, square = (row[:, i : i + 1] for i in range(3))
     alpha = rz / curvature
     beta = alpha * alpha * square / rz - 1.0
@@ -660,7 +667,7 @@
             tiles(9, 5), pltpu.VMEM((4, 16, 128), f32), rows(16), rows(16), rows(16),
             pltpu.VMEM((9, 3, 2, 16, 128), f32), tiles(8, 3), tiles(9),
             tiles(3), tiles(3), tiles(3), pltpu.VMEM((3, 1, 128), f32), tiles(2), tiles(), tiles(),
-            rows(2 * shape[1]), rows(ring), rows(2),
+            rows(2 * shape[1]), pltpu.VMEM((ring, 1, 128), f32), rows(2),
             dma((3,)), dma((8,)), dma((8,)), dma((2,)), dma((2,)), dma((5,)), dma((5,)), dma((2,)), dma((2,)),
             pltpu.SemaphoreType.REGULAR((4,)),
         ],

time: 50.4 us -> 50.1 us (level)
  no operation moved by 1% of the time
where the time goes in v4:
time: 50.1 us; the launch traced here: 49.9 us
  Pallas kernels  49.3 us (98%)
  between operations  0.64 us (1%)
    pallas_call x1, Pallas kernels, on_device(): pl.pallas_call(functools.partial(kernel, shape), out_shape=(out, out, out...  48.6 us

profile of v4, /device:TPU:1, one launch (start us, length us, event | category | flops | bytes accessed | tf_op | source)
XLA Modules:
  0.0 49.9 jit_solution(16158430478738062094)
XLA Ops:
  0.6 48.6 %step.1 = (f32[3,8,8,128]{3,2,1,0:T(8,128)S(1)}, f32[3,8,8,128]{3,2,1,0:T(8,128)S(1)}, f32[3,8,8,128]{3,2,1,0:T(8,128)S(1)}) custom-call(f32[3,8,8,128]{3,2,1,0:T(8,128)} %load_hbm.1, s32[7,7,127]{2,1,0:T(8,128)} %classes_hbm.1, f32[1,64]{1,0:T(1,128)} %bitcast.1), custom_call_target="tpu_custom_call" | custom-call | tf_op jit(solution)/shard_map/step/pallas_call | solution.py:658
  49.2 0.7 %store.1 = (f32[3,8,8,128]{3,2,1,0:T(8,128)}, f32[3,8,8,128]{3,2,1,0:T(8,128)}, f32[3,8,8,128]{3,2,1,0:T(8,128)}) custom-call(f32[3,8,8,128]{3,2,1,0:T(8,128)S(1)} %get-tuple-element.6.a_ref, f32[3,8,8,128]{3,2,1,0:T(8,128)S(1)} %get-tuple-element.7.b_ref, f32[3,8,8,128]{3,2,1,0:T(8,128)S(1)} %get-tuple-element.8.c_ref), custom_call_target="tpu_custom_call" | custom-call | tf_op jit(solution)/shard_map/store/pallas_call | solution.py:677

commit v5 on v4

--- a/solution.py
+++ b/solution.py
@@ -203,6 +203,14 @@
         (-1, -1): CLL, (-1, 1): CLU, (1, -1): CUL, (1, 1): CUU,
     }
 
+    loads = [
+        pltpu.make_async_copy(classes_hbm, classes_v, in_sem.at[0]),
+        pltpu.make_async_copy(densities_hbm, table_v, in_sem.at[1]),
+        pltpu.make_async_copy(load_hbm, load_v, in_sem.at[2]),
+    ]
+    for copy in loads:
+        copy.start()
+
     for (dy, dz), buffer in side_buffer.items():
         @pl.when(jnp.logical_not(both(dy, dz)))
         def _(buffer=buffer):
@@ -214,7 +222,8 @@
     def tell(device, semaphore):
         pl.semaphore_signal(semaphore, inc=1, device_id=device, device_id_type=MESH)
 
-    near = [ring_device(o, flip) for o in sorted({1, 2, ring - 1, ring - 2}) for flip in (False, True)]
+    two_away = [ring_device(o, flip) for o in sorted({2, ring - 2}) for flip in (False, True)]
+    one_away = [ring_device(o) for o in (1, -1)] if ring > 2 else []
     if NGY == 16:
         plane = [plane_device(*o) for o in ((0, 1), (0, 3), (1, 0), (3, 0))]
         plane_far = [plane_device(*o) for o in ((0, 2), (2, 0))]
@@ -241,22 +250,24 @@
         tell(block_device(1, 0, 0), barrier)
 
     awaited = jnp.logical_and(gives_left, core == 0).astype(jnp.int32)
-    for dy, dz in sorted(sides, key=lambda side: -abs(side[0]) - abs(side[1])):
+
+    def tell_side(dy, dz):
         @pl.when(both(dy, dz))
-        def _(dy=dy, dz=dz):
+        def _():
             tell(block_device(0, dy, dz), barrier)
-        awaited = awaited + both(dy, dz).astype(jnp.int32)
-    for device in near + plane + [flipped]:
+        return both(dy, dz).astype(jnp.int32)
+
+    for dy, dz in sides:
+        if dy and dz:
+            awaited = awaited + tell_side(dy, dz)
+    for device in two_away:
         tell(device, barrier)
-        awaited = awaited + 1
-
-    loads = [
-        pltpu.make_async_copy(classes_hbm, classes_v, in_sem.at[0]),
-        pltpu.make_async_copy(densities_hbm, table_v, in_sem.at[1]),
-        pltpu.make_async_copy(load_hbm, load_v, in_sem.at[2]),
-    ]
-    for copy in loads:
-        copy.start()
+    for dy, dz in sides:
+        if not (dy and dz):
+            awaited = awaited + tell_side(dy, dz)
+    for device in plane + one_away + [flipped]:
+        tell(device, barrier)
+    awaited = awaited + len(two_away + plane + one_away + [flipped])
 
     lane = lax.broadcasted_iota(jnp.int32, (8, 128), 1)
     sub = lax.broadcasted_iota(jnp.int32, (8, 128), 0)

time: 50.1 us -> 50.1 us (level)
  no operation moved by 1% of the time
where the time goes in v5:
time: 50.1 us; the launch traced here: 49.9 us
  Pallas kernels  49.3 us (98%)
  between operations  0.64 us (1%)
    pallas_call x1, Pallas kernels, on_device(): pl.pallas_call(functools.partial(kernel, shape), out_shape=(out, out, out...  48.6 us

profile of v5, /device:TPU:1, one launch (start us, length us, event | category | flops | bytes accessed | tf_op | source)
XLA Modules:
  0.0 49.9 jit_solution(14722325385172014253)
XLA Ops:
  0.6 48.6 %step.1 = (f32[3,8,8,128]{3,2,1,0:T(8,128)S(1)}, f32[3,8,8,128]{3,2,1,0:T(8,128)S(1)}, f32[3,8,8,128]{3,2,1,0:T(8,128)S(1)}) custom-call(f32[3,8,8,128]{3,2,1,0:T(8,128)} %load_hbm.1, s32[7,7,127]{2,1,0:T(8,128)} %classes_hbm.1, f32[1,64]{1,0:T(1,128)} %bitcast.1), custom_call_target="tpu_custom_call" | custom-call | tf_op jit(solution)/shard_map/step/pallas_call | solution.py:669
  49.2 0.7 %store.1 = (f32[3,8,8,128]{3,2,1,0:T(8,128)}, f32[3,8,8,128]{3,2,1,0:T(8,128)}, f32[3,8,8,128]{3,2,1,0:T(8,128)}) custom-call(f32[3,8,8,128]{3,2,1,0:T(8,128)S(1)} %get-tuple-element.6.a_ref, f32[3,8,8,128]{3,2,1,0:T(8,128)S(1)} %get-tuple-element.7.b_ref, f32[3,8,8,128]{3,2,1,0:T(8,128)S(1)} %get-tuple-element.8.c_ref), custom_call_target="tpu_custom_call" | custom-call | tf_op jit(solution)/shard_map/store/pallas_call | solution.py:688

commit v6 on v5

--- a/solution.py
+++ b/solution.py
@@ -100,12 +100,11 @@
     def field(f):
         return jnp.where(first, roll(lower, -27 * f, 1), roll(upper, 61 - 27 * f, 1))
 
-    s = jnp.zeros((16, 128), jnp.float32)
-    row = lax.broadcasted_iota(jnp.int32, (16, 128), 0)
+    s = jnp.zeros((8, 128), jnp.float32)
     for z in range(8):
-        found = jnp.where(first, roll(lower, z - 108, 1), roll(upper, z - 111 + 64, 1))
-        s = jnp.where(jnp.logical_and(layer == z, column < 2), found, s)
-    s = jnp.where(row < 8, s, 0.0)
+        found = jnp.where(first[0:8], roll(lower[0:8], z - 108, 1), roll(upper[0:8], z - 111 + 64, 1))
+        s = jnp.where(jnp.logical_and(layer[0:8] == z, column[0:8] < 2), found, s)
+    s = jnp.concatenate([s, jnp.zeros((8, 128), jnp.float32)], axis=0)
     d = shared(field(3))
     inv = inverse(d)
     starts, vectors, u = [], [], {}
@@ -139,16 +138,25 @@
         rz = rz + jnp.where(counted, starts[c] * vectors[c], 0.0)
         curvature = curvature + jnp.where(counted, vectors[c] * image, 0.0)
         square = square + jnp.where(counted, image * scaled, 0.0)
-        moved = jnp.where(first, roll(starts[c], -2, 1), roll(starts[c], 2, 1))
-        parts.append(jnp.where(column == jnp.where(first, 0, 2), moved, image)[0:8])
-    parts.append(d[0:8])
-    lane8 = lane[0:8]
+        parts.append((image[0:8], starts[c][0:8]))
+    return (rz, curvature, square), (parts, d[0:8])
+
+
+def strip_results(parts, d):
+    lane = lax.broadcasted_iota(jnp.int32, (8, 128), 1)
+    first = lane < 64
+    column = lax.rem(lax.rem(lane, 64), 3)
+    tiles = []
+    for image, start in parts:
+        moved = jnp.where(first, roll(start, -2, 1), roll(start, 2, 1))
+        tiles.append(jnp.where(column == jnp.where(first, 0, 2), moved, image))
+    tiles.append(d)
     for_lower = for_upper = jnp.zeros((8, 128), jnp.float32)
-    for i, part in enumerate(parts):
-        here = lax.div(lane8, 24) == i
-        for_lower = jnp.where(here, roll(part, 24 * i, 1), for_lower)
-        for_upper = jnp.where(here, roll(part, 24 * i - 64, 1), for_upper)
-    return (rz, curvature, square), for_lower, for_upper
+    for i, tile in enumerate(tiles):
+        here = lax.div(lane, 24) == i
+        for_lower = jnp.where(here, roll(tile, 24 * i, 1), for_lower)
+        for_upper = jnp.where(here, roll(tile, 24 * i - 64, 1), for_upper)
+    return for_lower, for_upper
 
 
 def kernel(
@@ -499,7 +507,7 @@
         jnp.logical_and(has_face, jnp.where(lane16 < 64, column, 2 - 2 * jnp.abs(column - 1)) > 0),
     )
     received = SR[...]
-    sums, for_lower, for_upper = strip_sums(
+    sums, found = strip_sums(
         jnp.where(mirrored, received, SL[...]), jnp.where(mirrored, SU[...], received), counted
     )
     rz, curvature, square = (
@@ -519,6 +527,7 @@
                 slot = k + (NGY if flip else 0)
                 remote(rows_v.at[pl.ds(0, 1)], RA.at[pl.ds(slot, 1)], a_send, a_recv, 0, device).start()
 
+    for_lower, for_upper = strip_results(*found)
     RS[0] = for_lower
     RS[1] = for_upper
     result_right = remote(RS.at[1], LOW, f_send, f_recv, 3, block_device(1, 0, 0))

time: 50.1 us -> 50.1 us (level)
  no operation moved by 1% of the time
where the time goes in v6:
time: 50.1 us; the launch traced here: 49.9 us
  Pallas kernels  49.3 us (98%)
  between operations  0.64 us (1%)
    pallas_call x1, Pallas kernels, on_device(): pl.pallas_call(functools.partial(kernel, shape), out_shape=(out, out, out...  48.6 us

profile of v6, /device:TPU:1, one launch (start us, length us, event | category | flops | bytes accessed | tf_op | source)
XLA Modules:
  0.0 49.9 jit_solution(8897560962715175353)
XLA Ops:
  0.6 48.6 %step.1 = (f32[3,8,8,128]{3,2,1,0:T(8,128)S(1)}, f32[3,8,8,128]{3,2,1,0:T(8,128)S(1)}, f32[3,8,8,128]{3,2,1,0:T(8,128)S(1)}) custom-call(f32[3,8,8,128]{3,2,1,0:T(8,128)} %load_hbm.1, s32[7,7,127]{2,1,0:T(8,128)} %classes_hbm.1, f32[1,64]{1,0:T(1,128)} %bitcast.1), custom_call_target="tpu_custom_call" | custom-call | tf_op jit(solution)/shard_map/step/pallas_call | solution.py:678
  49.2 0.7 %store.1 = (f32[3,8,8,128]{3,2,1,0:T(8,128)}, f32[3,8,8,128]{3,2,1,0:T(8,128)}, f32[3,8,8,128]{3,2,1,0:T(8,128)}) custom-call(f32[3,8,8,128]{3,2,1,0:T(8,128)S(1)} %get-tuple-element.6.a_ref, f32[3,8,8,128]{3,2,1,0:T(8,128)S(1)} %get-tuple-element.7.b_ref, f32[3,8,8,128]{3,2,1,0:T(8,128)S(1)} %get-tuple-element.8.c_ref), custom_call_target="tpu_custom_call" | custom-call | tf_op jit(solution)/shard_map/store/pallas_call | solution.py:697
